TPU v7x, 1024 devices: a whole 4x4x32 slice. The times are simulated.
1024 devices in a mesh: dp: 4 (over x_hi, core), shard: 256 (over y, z, x_lo).
Axes of the slice: x: 4 (x_hi: 2, x_lo: 2; x = x_hi * 2 + x_lo), y: 4, z: 32, core: 2. Of those that a mesh axis runs over, the one named last changes fastest.
Arguments:
- activations: bfloat16 [131072, 4096], P(('dp', 'shard')), may hold values from -24 to 24
- w_query: bfloat16 [4096, 128], P('shard'), may hold values from -0.09375 to 0.09375
- w_key: bfloat16 [4096, 128], P('shard'), may hold values from -0.09375 to 0.09375
- grad_query: bfloat16 [131072, 128], P(('dp', 'shard')), may hold values from -12 to 12
- grad_key: bfloat16 [131072, 128], P(('dp', 'shard')), may hold values from -12 to 12
Outputs:
- query_out: bfloat16 [131072, 128], P(('dp', 'shard'))
- key_out: bfloat16 [131072, 128], P(('dp', 'shard'))
- grad_input: bfloat16 [131072, 4096], P(('dp', 'shard'))
- grad_w_query: float32 [4096, 128], P('shard')
- grad_w_key: float32 [4096, 128], P('shard')
All inputs are finite; a program needn't handle non-finite values.
Results may differ from a plain program's by a relative error of at most 0.001.
Values may be sent and summed in bfloat16 or wider, within the bound.
No kernel may reach another device: no remote copies, remote signals or barrier semaphores. Data moves between devices by JAX's collectives and lax.ppermute only.
A program may use at most 64 MiB of HBM per device.

v0:
```python
import math

import jax
import jax.numpy as jnp
from jax import lax
from jax.sharding import PartitionSpec as P


def body(activations, w_query, w_key, grad_query, grad_key):
    head_size = w_query.shape[1]
    local_weights = jnp.concatenate([w_query, w_key], axis=1)
    cotangent = jnp.concatenate([grad_query, grad_key], axis=1)
    weights = lax.all_gather(local_weights, "shard", axis=0, tiled=True)
    projected = jnp.dot(activations, weights, preferred_element_type=jnp.float32)
    grad_input = lax.dot_general(
        cotangent, weights, (((1,), (1,)), ((), ())), preferred_element_type=jnp.float32
    ).astype(jnp.bfloat16)
    query_out = projected[:, :head_size].astype(jnp.bfloat16)
    key_out = projected[:, head_size:].astype(jnp.bfloat16)
    partial_sum = lax.dot_general(
        activations, cotangent, (((0,), (0,)), ((), ())), preferred_element_type=jnp.float32
    )
    replicas = lax.axis_size("dp")
    owners = lax.axis_size("shard")
    factor = 1.0 / math.sqrt(activations.shape[0] * replicas * owners)
    owned = lax.psum_scatter(partial_sum, "shard", scatter_dimension=0, tiled=True)
    summed = lax.psum(owned, "dp")
    summed = summed * factor
    return (query_out, key_out, grad_input, summed[:, :head_size], summed[:, head_size:])


def solution(mesh):
    placed = (
        P(("dp", "shard"), None),
        P("shard", None),
        P("shard", None),
        P(("dp", "shard"), None),
        P(("dp", "shard"), None),
    )
    return jax.shard_map(
        body,
        mesh=mesh,
        in_specs=placed,
        out_specs=(
            P(("dp", "shard"), None),
            P(("dp", "shard"), None),
            P(("dp", "shard"), None),
            P("shard", None),
            P("shard", None),
        ),
        check_vma=False,
    )
```

profile of v0, /device:TPU:1, one launch (start us, length us, event | category | flops | bytes accessed | tf_op | source)
XLA Modules:
  0.0 2436.8 jit_solution(4733855952608863598)
XLA Ops:
  7.2 0.0 copy-start
  7.2 0.0 all-gather.2.cloned.1.call-start
  7.2 1.4 pad_maximum_fusion
  8.6 0.0 all-gather.2.cloned.1.call-update
  8.6 0.0 reduce-scatter.4.cloned.1.call-start
  8.7 0.8 constant_dynamic-update-slice_fusion.1
  9.5 0.8 constant_dynamic-update-slice_fusion
  10.2 0.0 copy-done
  10.2 2.7 convolution_bitcast_fusion
  12.9 5.6 copy.18
  18.5 0.0 reduce-scatter.4.cloned.1.call-update
  18.5 985.4 %all-gather.2.cloned.1.call-done = bf16[4096,256]{1,0:T(8,128)(2,1)} async-done(((bf16[16,256]{1,0:T(8,128)(2,1)}), bf16[4096,256]{1,0:T(8,128)(2,1)}) %all-gather.2.cloned.1.call-update) | async-done | bytes 2097168 | tf_op jit(solution)/shard_map/all_gather | solution.py:13
  1003.9 0.0 copy-start.1
  1003.9 2.5 fusion
  1006.4 0.7 copy.14
  1007.2 0.7 copy.15
  1007.9 0.0 copy-done.1
  1007.9 1.8 convolution_convert_fusion
  1009.7 1192.8 %reduce-scatter.4.cloned.1.call-done = f32[16,256]{1,0:T(8,128)} async-done(((f32[4096,256]{1,0:T(8,128)}), f32[16,256]{1,0:T(8,128)}) %reduce-scatter.4.cloned.1.call-update) | async-done | bytes 16400
  2202.5 0.8 copy.19
  2203.3 225.3 %psum.7 = f32[16,256]{0,1:T(8,128)S(1)} all-reduce(f32[16,256]{0,1:T(8,128)S(1)} %copy.19), channel_id=1, replica_groups=mesh['dp'=4,'shard'=256] {'dp'}, use_global_device_ids=true, to_apply=%region_1.0 | all-reduce | flops 4096 | bytes 32768 | tf_op jit(solution)/shard_map/psum | solution.py:27
  2428.6 0.7 copy.16
  2429.3 0.7 copy.17
  (3 shorter events, 0.0 us)
Async XLA Ops:
  7.2 3.1 copy-start
  7.2 996.7 %all-gather.2.cloned.1.call-start = ((), (), s32[]{:S(2)}) async-start(), calls=%async_computation.1 | async-start | bytes 2105344 | tf_op jit(solution)/shard_map/all_gather | solution.py:13
  8.6 2193.9 %reduce-scatter.4.cloned.1.call-start = ((), (), s32[]{:S(2)}) async-start(), calls=%async_computation.2 | async-start | bytes 4210688
  1003.9 4.0 copy-start.1
Sparse Core Ops, SparseCore 0:
  11.3 992.6 all-gather.1
  1007.3 1195.1 reduce-scatter.3
where the time goes:
time: 2440 us
  waiting for transfers between devices  2180 us (89%)
  blocking collectives  225 us (9%)
    unnamed x3, waiting for transfers between devices  1190 us
    all_gather x1, waiting for transfers between devices, body(): weights = lax.all_gather(local_weights, 'shard', axis=0, tiled=True)  985 us
    psum x1, blocking collectives, body(): summed = lax.psum(owned, 'dp')  225 us
  transfers between devices with their start and end apart: 2, of which 2 were waited for; matrix products, arithmetic and copies ran while one was open for 1% of the time, Pallas kernels for 0%

commit v1 on v0

v1 whole, which is shorter than its diff:
```python
import math

import jax
import jax.numpy as jnp
from jax import lax
from jax.sharding import Mesh, PartitionSpec as P

PLANE = ("xh", "y", "xl")


def swap_cores(block):
    return lax.ppermute(block, "c", [(0, 1), (1, 0)])


def pick(first, second):
    return lax.select(lax.axis_index("c") == 0, first, second)


def spread(block, axes, count):
    copies = jnp.broadcast_to(block[None], (count,) + block.shape)
    return lax.all_to_all(copies, axes, 0, 0, tiled=True)


def body(activations, w_query, w_key, grad_query, grad_key):
    width = activations.shape[1]
    head = w_query.shape[1]
    xh, cores, ys, zs, xl = (lax.axis_size(a) for a in ("xh", "c", "y", "z", "xl"))
    rows = w_query.shape[0]
    half = rows // xh
    plane = xh * ys * xl
    tokens = activations.shape[0] * plane * cores * zs
    factor = 1.0 / math.sqrt(tokens)

    def terms(cotangent):
        return lax.dot_general(
            activations, cotangent, (((0,), (0,)), ((), ())), preferred_element_type=jnp.float32
        )

    mine = pick(grad_query, grad_key)
    other = pick(grad_key, grad_query)
    arrived = swap_cores(terms(other))
    own = pick(w_query, w_key)
    own = lax.dynamic_slice_in_dim(own, lax.axis_index("xh") * half, half, 0)
    column = spread(own, "z", zs)
    sheet = spread(column, PLANE, plane)
    sheet = sheet.reshape(xh, ys, xl, zs, half, head).transpose(1, 3, 2, 0, 4, 5).reshape(width, head)
    other_sheet = swap_cores(sheet)
    wq = pick(sheet, other_sheet)
    wk = pick(other_sheet, sheet)

    paired = terms(mine) + arrived
    paired = paired.reshape(ys, zs, xl, xh, half, head).transpose(3, 0, 2, 1, 4, 5)
    paired = paired.reshape(plane, zs, half, head)
    summed = lax.all_to_all(paired, PLANE, 0, 0, tiled=True).sum(axis=0)
    summed = lax.all_to_all(summed, "z", 0, 0, tiled=True).sum(axis=0) * factor
    whole = lax.all_gather(summed, ("c", "xh"), axis=0, tiled=True)

    weights = jnp.concatenate([wq, wk], axis=1)
    cotangent = jnp.concatenate([grad_query, grad_key], axis=1)
    projected = jnp.dot(activations, weights, preferred_element_type=jnp.float32).astype(jnp.bfloat16)
    grad_input = lax.dot_general(
        cotangent, weights, (((1,), (1,)), ((), ())), preferred_element_type=jnp.float32
    ).astype(jnp.bfloat16)
    return (projected[:, :head], projected[:, head:], grad_input, whole[:rows], whole[rows:])


def solution(mesh):
    shape = (2, 2, 4, mesh.shape["shard"] // 8, 2)
    fine = Mesh(mesh.devices.reshape(shape), ("xh", "c", "y", "z", "xl"))
    tokens = P(("xh", "c", "y", "z", "xl"), None)
    weights = P(("y", "z", "xl"), None)
    return jax.shard_map(
        body,
        mesh=fine,
        in_specs=(tokens, weights, weights, tokens, tokens),
        out_specs=(tokens, tokens, tokens, weights, weights),
        check_vma=False,
    )
```

time: 2440 us -> 169 us (0.07)
  waiting for transfers between devices: 2180 us -> 52.9 us
  blocking collectives: 225 us -> 57.6 us
  starting transfers between devices: 0.08 us -> 36.6 us
    unnamed x3 -> x0, waiting for transfers between devices: 1190 us -> none
    all_gather x1 -> x0, waiting for transfers between devices: 985 us -> none  [body(): weights = lax.all_gather(local_weights, 'shard', axis=0, tiled=True)]
    psum x1 -> x0, blocking collectives: 225 us -> none  [body(): summed = lax.psum(owned, 'dp')]
    all_to_all x0 -> x3, waiting for transfers between devices: none -> 52.9 us  [the longest x1 24 us: body(): summed = lax.all_to_all(paired, PLANE, 0, 0, tiled=True).sum(axis=0)]
    all_to_all x0 -> x1, blocking collectives: none -> 40.4 us  [spread(): return lax.all_to_all(copies, axes, 0, 0, tiled=True)]
  transfers between devices with their start and end apart: 2 -> 5, of which waited for: 2 -> 3; matrix products, arithmetic and copies ran while one was open for 1% -> 10% of each run, Pallas kernels for 0% -> 0%
where the time goes in v1:
time: 169 us; the launch traced here: 168 us
  blocking collectives  57.6 us (34%)
  waiting for transfers between devices  52.9 us (31%)
  starting transfers between devices  36.6 us (22%)
  local copies, waits for them, and re-layouts  11.8 us (7%)
  matrix products  5.81 us (3%)
  other arithmetic  2.48 us (1%)
    all_to_all x1, blocking collectives, spread(): return lax.all_to_all(copies, axes, 0, 0, tiled=True)  40.4 us
    all_to_all x1, waiting for transfers between devices, body(): summed = lax.all_to_all(paired, PLANE, 0, 0, tiled=True).sum(axis=0)  24 us
    all_to_all x1, waiting for transfers between devices, body(): summed = lax.all_to_all(summed, 'z', 0, 0, tiled=True).sum(axis=0) * factor  21.2 us
    ppermute x2, starting transfers between devices, swap_cores(): return lax.ppermute(block, 'c', [(0, 1), (1, 0)])  19.1 us
    all_gather x1, blocking collectives, body(): whole = lax.all_gather(summed, ('c', 'xh'), axis=0, tiled=True)  17.2 us
    all_to_all x1, waiting for transfers between devices, spread(): return lax.all_to_all(copies, axes, 0, 0, tiled=True)  7.73 us
    all_to_all x1, starting transfers between devices, spread(): return lax.all_to_all(copies, axes, 0, 0, tiled=True)  6.81 us
    all_to_all x1, starting transfers between devices, body(): summed = lax.all_to_all(paired, PLANE, 0, 0, tiled=True).sum(axis=0)  6.72 us
  transfers between devices with their start and end apart: 5, of which 3 were waited for; matrix products, arithmetic and copies ran while one was open for 10% of the time, Pallas kernels for 0%

profile of v1, /device:TPU:1, one launch (start us, length us, event | category | flops | bytes accessed | tf_op | source)
XLA Modules:
  0.0 168.0 jit_solution(15878231128195436076)
XLA Ops:
  0.7 1.2 copy-done
  1.9 1.2 convolution_bitcast_fusion
  3.1 16.1 %collective-permute-start.1 = (f32[4096,128]{0,1:T(8,128)S(1)}, f32[4096,128]{0,1:T(8,128)}, u32[]{:S(2)}, u32[]{:S(2)}) collective-permute-start(f32[4096,128]{0,1:T(8,128)S(1)} %convolution_bitcast_fusion), channel_id=1, source_target_pairs={{0,256},{256,0},{1,257},{257,1},{2,258},{258,2},{3,259},{259,3},{4... | collective-permute-start | bytes 6291464 | tf_op jit(solution)/shard_map/ppermute | solution.py:12
  19.3 40.4 %all_to_all.20 = bf16[32,8,128]{2,1,0:T(8,128)(2,1)S(1)} all-to-all(bf16[32,8,128]{2,1,0:T(8,128)(2,1)S(1)} %broadcast_in_dim.4), channel_id=1, replica_groups=mesh['xh'=2,'c'=2,'y'=4,'z'=32,'xl'=2] {'z'}, dimensions={0} | all-to-all | bytes 131072 | tf_op jit(solution)/shard_map/all_to_all | solution.py:21
  59.6 1.2 broadcast_in_dim.5
  60.8 6.8 %all-to-all-start.1 = ((bf16[16,32,8,128]{3,2,1,0:T(8,128)(2,1)}), bf16[16,32,8,128]{3,2,1,0:T(8,128)(2,1)}, u32[]{:S(2)}, u32[]{:S(2)}) async-start(bf16[16,32,8,128]{3,2,1,0:T(8,128)(2,1)} %broadcast_in_dim.5), calls=%async_computation.1 | async-start | bytes 2097152 | tf_op jit(solution)/shard_map/all_to_all | solution.py:21
  67.6 2.1 %fusion = f32[4096,128]{0,1:T(8,128)S(1)} fusion(f32[4096,128]{0,1:T(8,128)} %collective-permute-done.1, bf16[128,4096]{1,0:T(8,128)(2,1)S(1)} %copy-done, bf16[128,128]{1,0:T(8,128)(2,1)S(1)} %copy-done.2, bf16[128,128]{1,0:T(8,128)(2,1)S(1)} %copy-done.1, pred[]{:T(512)S(6)} %eq.2), kind=kOutput, calls=%fused_computation.2 | convolution fusion | flops 134758400 | bytes 5308417 | tf_op jit(solution)/shard_map/dot_general | solution.py:35
  69.7 1.8 %copy.22 = f32[4096,128]{1,0:T(8,128)} copy(f32[4096,128]{0,1:T(8,128)S(1)} %fusion) | data formatting | bytes 4194304 | tf_op jit(solution)/shard_map/add | solution.py:51
  71.5 3.2 %copy.23 = f32[2,4,2,32,8,128]{5,4,3,2,1,0:T(8,128)} copy(f32[2,4,2,32,8,128]{5,4,0,2,3,1:T(8,128)} %bitcast.21) | data formatting | bytes 4194304 | tf_op jit(solution)/shard_map/transpose | solution.py:52
  74.7 7.7 %all-to-all-done.1 = bf16[16,32,8,128]{3,2,1,0:T(8,128)(2,1)} async-done(((bf16[16,32,8,128]{3,2,1,0:T(8,128)(2,1)}), bf16[16,32,8,128]{3,2,1,0:T(8,128)(2,1)}, u32[]{:S(2)}, u32[]{:S(2)}) %all-to-all-start.1) | async-done | bytes 1048608 | tf_op jit(solution)/shard_map/all_to_all | solution.py:21
  82.4 6.7 %all-to-all-start.2 = ((f32[16,32,8,128]{3,2,1,0:T(8,128)}), f32[16,32,8,128]{3,2,1,0:T(8,128)S(1)}, u32[]{:S(2)}, u32[]{:S(2)}) async-start(f32[16,32,8,128]{3,2,1,0:T(8,128)} %bitcast.8), calls=%async_computation.2 | async-start | bytes 4194304 | tf_op jit(solution)/shard_map/all_to_all | solution.py:54
  89.1 2.4 %copy.21 = bf16[4,32,2,2,8,128]{5,4,3,2,1,0:T(8,128)(2,1)} copy(bf16[4,32,2,2,8,128]{5,4,1,2,0,3:T(8,128)(2,1)} %bitcast.1) | data formatting | bytes 2097152 | tf_op jit(solution)/shard_map/transpose | solution.py:46
  91.5 3.1 %collective-permute-start = (bf16[4096,128]{1,0:T(8,128)(2,1)}, bf16[4096,128]{1,0:T(8,128)(2,1)}, u32[]{:S(2)}, u32[]{:S(2)}) collective-permute-start(bf16[4096,128]{1,0:T(8,128)(2,1)} %bitcast.2), channel_id=1, source_target_pairs={{0,256},{256,0},{1,257},{257,1},{2,258},{258,2},{3,259},{259,3},{4... | collective-permute-start | bytes 3145736 | tf_op jit(solution)/shard_map/ppermute | solution.py:12
  94.6 24.0 %all-to-all-done.2 = f32[16,32,8,128]{3,2,1,0:T(8,128)S(1)} async-done(((f32[16,32,8,128]{3,2,1,0:T(8,128)}), f32[16,32,8,128]{3,2,1,0:T(8,128)S(1)}, u32[]{:S(2)}, u32[]{:S(2)}) %all-to-all-start.2) | async-done | bytes 2097184 | tf_op jit(solution)/shard_map/all_to_all | solution.py:54
  118.6 0.7 reduce_sum.18
  119.3 3.9 %all-to-all-start.3 = ((f32[32,8,128]{2,1,0:T(8,128)}), f32[32,8,128]{2,1,0:T(8,128)S(1)}, u32[]{:S(2)}, u32[]{:S(2)}) async-start(f32[32,8,128]{2,1,0:T(8,128)} %reduce_sum.18), calls=%async_computation.3 | async-start | bytes 262144 | tf_op jit(solution)/shard_map/all_to_all | solution.py:55
  123.3 1.7 %broadcast_select_fusion.1 = (bf16[4096,128]{1,0:T(8,128)(2,1)S(1)}, bf16[4096,128]{1,0:T(8,128)(2,1)S(1)}) fusion(bf16[4096,128]{1,0:T(8,128)(2,1)} %collective-permute-done, pred[]{:T(512)S(6)} %eq.2, bf16[4,32,2,2,8,128]{5,4,3,2,1,0:T(8,128)(2,1)} %copy.21), kind=kLoop, calls=%fused_computation.9 | loop fusion | flops 1048576 | bytes 4194305 | tf_op jit(solution)/shard_map/select_n | solution.py:16
  125.0 0.8 fusion.3
  125.8 0.7 copy.25
  126.5 0.7 copy.24
  127.2 1.8 %convolution_convert_fusion = bf16[128,4096]{1,0:T(8,128)(2,1)} fusion(bf16[4096,128]{1,0:T(8,128)(2,1)S(1)} %get-tuple-element.26, bf16[4096,128]{1,0:T(8,128)(2,1)S(1)} %get-tuple-element.25, bf16[128,128]{1,0:T(8,128)(2,1)S(1)} %copy-done.1, bf16[128,128]{1,0:T(8,128)(2,1)S(1)} %copy-done.2), kind=kOutput, calls=%fused_computation.3 | convolution fusion | flops 273285120 | bytes 3211264 | tf_op jit(solution)/shard_map/dot_general | solution.py:61
  129.0 21.2 %all-to-all-done.3 = f32[32,8,128]{2,1,0:T(8,128)S(1)} async-done(((f32[32,8,128]{2,1,0:T(8,128)}), f32[32,8,128]{2,1,0:T(8,128)S(1)}, u32[]{:S(2)}, u32[]{:S(2)}) %all-to-all-start.3) | async-done | bytes 131104 | tf_op jit(solution)/shard_map/all_to_all | solution.py:55
  150.2 17.2 %all_gather.3 = f32[32,128]{1,0:T(8,128)S(1)} all-gather(f32[8,128]{1,0:T(8,128)S(1)} %broadcast_multiply_fusion), channel_id=1, replica_groups=mesh['xh'=2,'c'=2,'y'=4,'z'=32,'xl'=2] {'c','xh'}, dimensions={0}, use_global_device_ids=true | all-gather | bytes 20480 | tf_op jit(solution)/shard_map/all_gather | solution.py:56
  167.4 0.6 fusion.14
  (16 shorter events, 0.1 us)
Async XLA Ops:
  0.6 1.2 copy-start
  0.6 18.6 %copy-start.3 = (bf16[16,128]{1,0:T(8,128)(2,1)S(1)}, bf16[16,128]{1,0:T(8,128)(2,1)}, u32[]{:S(2)}) copy-start(bf16[16,128]{1,0:T(8,128)(2,1)} %param.7) | copy-start | bytes 12292
  0.7 18.6 %copy-start.4 = (bf16[16,128]{1,0:T(8,128)(2,1)S(1)}, bf16[16,128]{1,0:T(8,128)(2,1)}, u32[]{:S(2)}) copy-start(bf16[16,128]{1,0:T(8,128)(2,1)} %param.6) | copy-start | bytes 12292
  3.1 64.5 %copy-start.1 = (bf16[128,128]{1,0:T(8,128)(2,1)S(1)}, bf16[128,128]{1,0:T(8,128)(2,1)}, u32[]{:S(2)}) copy-start(bf16[128,128]{1,0:T(8,128)(2,1)} %param.9) | copy-start | bytes 98308
  3.1 64.5 %copy-start.2 = (bf16[128,128]{1,0:T(8,128)(2,1)S(1)}, bf16[128,128]{1,0:T(8,128)(2,1)}, u32[]{:S(2)}) copy-start(bf16[128,128]{1,0:T(8,128)(2,1)} %param.8) | copy-start | bytes 98308
  3.1 64.5 %collective-permute-start.1 = (f32[4096,128]{0,1:T(8,128)S(1)}, f32[4096,128]{0,1:T(8,128)}, u32[]{:S(2)}, u32[]{:S(2)}) collective-permute-start(f32[4096,128]{0,1:T(8,128)S(1)} %convolution_bitcast_fusion), channel_id=1, source_target_pairs={{0,256},{256,0},{1,257},{257,1},{2,258},{258,2},{3,259},{259,3},{4... | collective-permute-start | bytes 6291464 | tf_op jit(solution)/shard_map/ppermute | solution.py:12
  60.8 21.6 %all-to-all-start.1 = ((bf16[16,32,8,128]{3,2,1,0:T(8,128)(2,1)}), bf16[16,32,8,128]{3,2,1,0:T(8,128)(2,1)}, u32[]{:S(2)}, u32[]{:S(2)}) async-start(bf16[16,32,8,128]{3,2,1,0:T(8,128)(2,1)} %broadcast_in_dim.5), calls=%async_computation.1 | async-start | bytes 2097152 | tf_op jit(solution)/shard_map/all_to_all | solution.py:21
  82.4 36.2 %all-to-all-start.2 = ((f32[16,32,8,128]{3,2,1,0:T(8,128)}), f32[16,32,8,128]{3,2,1,0:T(8,128)S(1)}, u32[]{:S(2)}, u32[]{:S(2)}) async-start(f32[16,32,8,128]{3,2,1,0:T(8,128)} %bitcast.8), calls=%async_computation.2 | async-start | bytes 4194304 | tf_op jit(solution)/shard_map/all_to_all | solution.py:54
  91.5 31.8 %collective-permute-start = (bf16[4096,128]{1,0:T(8,128)(2,1)}, bf16[4096,128]{1,0:T(8,128)(2,1)}, u32[]{:S(2)}, u32[]{:S(2)}) collective-permute-start(bf16[4096,128]{1,0:T(8,128)(2,1)} %bitcast.2), channel_id=1, source_target_pairs={{0,256},{256,0},{1,257},{257,1},{2,258},{258,2},{3,259},{259,3},{4... | collective-permute-start | bytes 3145736 | tf_op jit(solution)/shard_map/ppermute | solution.py:12
  119.3 30.8 %all-to-all-start.3 = ((f32[32,8,128]{2,1,0:T(8,128)}), f32[32,8,128]{2,1,0:T(8,128)S(1)}, u32[]{:S(2)}, u32[]{:S(2)}) async-start(f32[32,8,128]{2,1,0:T(8,128)} %reduce_sum.18), calls=%async_computation.3 | async-start | bytes 262144 | tf_op jit(solution)/shard_map/all_to_all | solution.py:55

commit v2 on v1

v2 whole, which is shorter than its diff:
```python
import math

import jax
import jax.numpy as jnp
from jax import lax
from jax.experimental import pallas as pl
from jax.experimental.pallas import tpu as pltpu
from jax.sharding import Mesh, PartitionSpec as P

PLANE = ("xh", "y", "xl")


def swap_cores(block):
    return lax.ppermute(block, "c", [(0, 1), (1, 0)])


def pick(first, second):
    return lax.select(lax.axis_index("c") == 0, first, second)


def terms_kernel(act_ref, cot_ref, *refs):
    out_ref = refs[-1]
    xh, _, xl, zs, half, head = out_ref.shape
    part = lax.dot_general(
        act_ref[...], cot_ref[...], (((0,), (0,)), ((), ())), preferred_element_type=jnp.float32
    ).reshape(zs, xl, xh, half, head)
    for i in range(xh):
        for j in range(xl):
            piece = part[:, j, i]
            if len(refs) == 2:
                piece = piece + refs[0][i, 0, j]
            out_ref[i, 0, j] = piece


def terms(activations, cotangent, arrived=None):
    tokens, width = activations.shape
    head = cotangent.shape[1]
    ys, zs = lax.axis_size("y"), lax.axis_size("z")
    cut = 2
    block = width // (ys * cut)
    half = width // (4 * ys * zs)
    spread = pl.BlockSpec((2, 1, 2, zs // cut, half, head), lambda y, z: (0, y, 0, z, 0, 0))
    operands = [activations, cotangent] + ([] if arrived is None else [arrived])
    return pl.pallas_call(
        terms_kernel,
        grid=(ys, cut),
        in_specs=[
            pl.BlockSpec((tokens, block), lambda y, z: (0, y * cut + z)),
            pl.BlockSpec((tokens, head), lambda y, z: (0, 0)),
        ]
        + [spread] * (len(operands) - 2),
        out_specs=spread,
        out_shape=jax.ShapeDtypeStruct((2, ys, 2, zs, half, head), jnp.float32),
        cost_estimate=pl.CostEstimate(
            flops=2 * tokens * width * head, bytes_accessed=6 * width * head, transcendentals=0
        ),
    )(*operands)


def body(activations, w_query, w_key, grad_query, grad_key):
    width = activations.shape[1]
    rows, head = w_query.shape
    ys, zs = lax.axis_size("y"), lax.axis_size("z")
    half = rows // 2
    plane = 4 * ys
    factor = 1.0 / math.sqrt(activations.shape[0] * 2 * plane * zs)

    mine = pick(grad_query, grad_key)
    other = pick(grad_key, grad_query)
    arrived = swap_cores(terms(activations, other))
    paired = terms(activations, mine, arrived).reshape(plane, zs, half, head)
    summed = lax.all_to_all(paired, PLANE, 0, 0, tiled=True).sum(axis=0)

    own = pick(w_query, w_key)
    own = lax.dynamic_slice_in_dim(own, lax.axis_index("xh") * half, half, 0)
    high = lax.reduce_precision(summed, 8, 7)
    low = summed - high
    sent = jnp.concatenate(
        [jnp.broadcast_to(own[None], (zs, half, head)), high.astype(jnp.bfloat16), low.astype(jnp.bfloat16)],
        axis=1,
    )
    landed = lax.all_to_all(sent, "z", 0, 0, tiled=True)
    column = landed[:, :half]
    summed = landed[:, half:].astype(jnp.float32)
    summed = (summed[:, :half] + summed[:, half:]).sum(axis=0) * factor

    sheet = lax.all_to_all(
        jnp.broadcast_to(column[None], (plane, zs, half, head)), PLANE, 0, 0, tiled=True
    )
    whole = lax.all_gather(summed, ("c", "xh"), axis=0, tiled=True)
    sheet = sheet.reshape(2, ys, 2, zs, half, head).transpose(1, 3, 2, 0, 4, 5).reshape(width, head)
    other_sheet = swap_cores(sheet)

    weights = jnp.concatenate([sheet, other_sheet], axis=1)
    cotangent = jnp.concatenate([mine, other], axis=1)
    projected = jnp.dot(activations, weights, preferred_element_type=jnp.float32).astype(jnp.bfloat16)
    grad_input = lax.dot_general(
        cotangent, weights, (((1,), (1,)), ((), ())), preferred_element_type=jnp.float32
    ).astype(jnp.bfloat16)
    first, second = projected[:, :head], projected[:, head:]
    return (pick(first, second), pick(second, first), grad_input, whole[:rows], whole[rows:])


def solution(mesh):
    names = ("xh", "c", "y", "z", "xl")
    shape = (2, 2, 4, mesh.shape["shard"] // 8, 2)
    fine = Mesh(mesh.devices.reshape(shape), names)
    tokens = P(names, None)
    weights = P(("y", "z", "xl"), None)
    return jax.shard_map(
        body,
        mesh=fine,
        in_specs=(tokens, weights, weights, tokens, tokens),
        out_specs=(tokens, tokens, tokens, weights, weights),
        check_vma=False,
    )
```

time: 169 us -> 167 us (0.988)
  blocking collectives: 57.6 us -> 86.3 us
  waiting for transfers between devices: 52.9 us -> 34.5 us
  Pallas kernels: 0 us -> 12.8 us
  starting transfers between devices: 36.6 us -> 25.3 us
  local copies, waits for them, and re-layouts: 11.8 us -> 2.36 us
  matrix products: 5.81 us -> 2.26 us
    all_to_all x1 -> x2, blocking collectives: 40.4 us -> 74.3 us  [the longest x1 52.8 us: body(): landed = lax.all_to_all(sent, 'z', 0, 0, tiled=True)]
    all_to_all x2 -> x0, waiting for transfers between devices: 28.9 us -> none  [the longest x1 21.2 us: body(): summed = lax.all_to_all(summed, 'z', 0, 0, tiled=True).sum(axis=0) * factor]
    pallas_call x0 -> x2, Pallas kernels: none -> 12.8 us  [terms(): pl.pallas_call(terms_kernel, grid=(ys, cut), in_specs=[pl.BlockSpec((toke...]
    all_to_all x2 -> x0, starting transfers between devices: 10.8 us -> none  [the longest x1 6.81 us: spread(): return lax.all_to_all(copies, axes, 0, 0, tiled=True)]
    all_to_all x1, waiting for transfers between devices: 24 us -> 30.5 us  [body(): summed = lax.all_to_all(paired, PLANE, 0, 0, tiled=True).sum(axis=0)]
    transpose x2 -> x1, local copies, waits for them, and re-layouts: 5.54 us -> 0.18 us  [body(): sheet.reshape(2, ys, 2, zs, half, head).transpose(1, 3, 2, 0, 4, 5)]
    all_gather x1, blocking collectives: 17.2 us -> 12 us  [body(): whole = lax.all_gather(summed, ('c', 'xh'), axis=0, tiled=True)]
    ppermute x2, waiting for transfers between devices: 0.01 us -> 3.98 us  [swap_cores(): return lax.ppermute(block, 'c', [(0, 1), (1, 0)])]
  transfers between devices with their start and end apart: 5 -> 3, of which waited for: 3 -> 2; matrix products, arithmetic and copies ran while one was open for 10% -> 0% of each run, Pallas kernels for 0% -> 0%
where the time goes in v2:
time: 167 us
  blocking collectives  86.3 us (52%)
  waiting for transfers between devices  34.5 us (21%)
  starting transfers between devices  25.3 us (15%)
  Pallas kernels  12.8 us (8%)
  local copies, waits for them, and re-layouts  2.36 us (1%)
  other arithmetic  2.28 us (1%)
  matrix products  2.26 us (1%)
    all_to_all x1, blocking collectives, body(): landed = lax.all_to_all(sent, 'z', 0, 0, tiled=True)  52.8 us
    all_to_all x1, waiting for transfers between devices, body(): summed = lax.all_to_all(paired, PLANE, 0, 0, tiled=True).sum(axis=0)  30.5 us
    all_to_all x1, blocking collectives, body(): lax.all_to_all(jnp.broadcast_to(column[None], (plane, zs, half, head)), P...  21.5 us
    ppermute x2, starting transfers between devices, swap_cores(): return lax.ppermute(block, 'c', [(0, 1), (1, 0)])  21.5 us
    pallas_call x2, Pallas kernels, terms(): pl.pallas_call(terms_kernel, grid=(ys, cut), in_specs=[pl.BlockSpec((toke...  12.8 us
    all_gather x1, blocking collectives, body(): whole = lax.all_gather(summed, ('c', 'xh'), axis=0, tiled=True)  12 us
    ppermute x2, waiting for transfers between devices, swap_cores(): return lax.ppermute(block, 'c', [(0, 1), (1, 0)])  3.98 us
    all_to_all x1, starting transfers between devices, body(): summed = lax.all_to_all(paired, PLANE, 0, 0, tiled=True).sum(axis=0)  3.85 us
  transfers between devices with their start and end apart: 3, of which 2 were waited for; matrix products, arithmetic and copies ran while one was open for 0% of the time, Pallas kernels for 0%

profile of v2, /device:TPU:1, one launch (start us, length us, event | category | flops | bytes accessed | tf_op | source)
XLA Modules:
  0.0 166.6 jit_solution(4815408453374381007)
XLA Ops:
  0.6 1.4 broadcast_select_fusion.2
  2.0 6.2 %shard_map.92 = f32[2,4,2,32,8,128]{5,4,3,2,1,0:T(8,128)} custom-call(bf16[128,4096]{1,0:T(8,128)(2,1)} %act_ref.3, bf16[128,128]{1,0:T(8,128)(2,1)} %get-tuple-element.9.cot_ref), custom_call_target="tpu_custom_call" | custom-call | flops 134217728 | bytes 3145728 | tf_op jit(solution)/shard_map/pallas_call | solution.py:44
  8.2 16.1 %collective-permute-start = (f32[2,4,2,32,8,128]{5,4,3,2,1,0:T(8,128)}, f32[2,4,2,32,8,128]{5,4,3,2,1,0:T(8,128)S(1)}, u32[]{:S(2)}, u32[]{:S(2)}) collective-permute-start(f32[2,4,2,32,8,128]{5,4,3,2,1,0:T(8,128)} %shard_map.92), channel_id=1, source_target_pairs={{0,256},{256,0},{1,257},{257,1},{2,258},{258,2},{3,259},{259,3},{4... | collective-permute-start | bytes 6291464 | tf_op jit(solution)/shard_map/ppermute | solution.py:14
  24.3 4.0 %collective-permute-done.refs_0_ = f32[2,4,2,32,8,128]{5,4,3,2,1,0:T(8,128)S(1)} collective-permute-done((f32[2,4,2,32,8,128]{5,4,3,2,1,0:T(8,128)}, f32[2,4,2,32,8,128]{5,4,3,2,1,0:T(8,128)S(1)}, u32[]{:S(2)}, u32[]{:S(2)}) %collective-permute-start) | collective-permute-done | bytes 2097184 | tf_op jit(solution)/shard_map/ppermute | solution.py:14
  28.2 1.3 copy-done.1
  29.6 6.6 %shard_map.93 = f32[2,4,2,32,8,128]{5,4,3,2,1,0:T(8,128)} custom-call(bf16[128,4096]{1,0:T(8,128)(2,1)} %act_ref.3, bf16[128,128]{1,0:T(8,128)(2,1)} %get-tuple-element.10.cot_ref, f32[2,4,2,32,8,128]{5,4,3,2,1,0:T(8,128)} %copy-done.1), custom_call_target="tpu_custom_call" | custom-call | flops 134217728 | bytes 3145728 | tf_op jit(solution)/shard_map/pallas_call | solution.py:44
  36.2 3.8 %all-to-all-start = ((f32[16,32,8,128]{3,2,1,0:T(8,128)}), f32[16,32,8,128]{3,2,1,0:T(8,128)S(1)}, u32[]{:S(2)}, u32[]{:S(2)}) async-start(f32[16,32,8,128]{3,2,1,0:T(8,128)} %bitcast.8), calls=%async_computation | async-start | bytes 4194304 | tf_op jit(solution)/shard_map/all_to_all | solution.py:72
  40.1 0.0 copy-done.4
  40.1 30.5 %all-to-all-done = f32[16,32,8,128]{3,2,1,0:T(8,128)S(1)} async-done(((f32[16,32,8,128]{3,2,1,0:T(8,128)}), f32[16,32,8,128]{3,2,1,0:T(8,128)S(1)}, u32[]{:S(2)}, u32[]{:S(2)}) %all-to-all-start) | async-done | bytes 2097184 | tf_op jit(solution)/shard_map/all_to_all | solution.py:72
  70.6 0.1 reduce_sum.18
  70.8 52.8 %all_to_all.15 = bf16[32,24,128]{2,1,0:T(8,128)(2,1)S(1)} all-to-all(bf16[32,24,128]{2,1,0:T(8,128)(2,1)S(1)} %pad_maximum_fusion.7), channel_id=1, replica_groups=mesh['xh'=2,'c'=2,'y'=4,'z'=32,'xl'=2] {'z'}, dimensions={0} | all-to-all | bytes 393216 | tf_op jit(solution)/shard_map/all_to_all | solution.py:82
  123.6 0.2 broadcast_in_dim.5
  123.8 0.0 copy-start
  123.9 21.5 %all_to_all.16 = bf16[16,32,8,128]{3,2,1,0:T(8,128)(2,1)S(1)} all-to-all(bf16[16,32,8,128]{3,2,1,0:T(8,128)(2,1)S(1)} %broadcast_in_dim.5), channel_id=1, replica_groups=mesh['xh'=2,'c'=2,'y'=4,'z'=32,'xl'=2] {'xh','y','xl'}, dimensions={0} | all-to-all | bytes 2097152 | tf_op jit(solution)/shard_map/all_to_all | solution.py:87
  145.4 0.2 copy.12
  145.6 5.4 %collective-permute-start.1 = (bf16[4096,128]{1,0:T(8,128)(2,1)S(1)}, bf16[4096,128]{1,0:T(8,128)(2,1)S(1)}, u32[]{:S(2)}, u32[]{:S(2)}) collective-permute-start(bf16[4096,128]{1,0:T(8,128)(2,1)S(1)} %bitcast.10), channel_id=1, source_target_pairs={{0,256},{256,0},{1,257},{257,1},{2,258},{258,2},{3,259},{259,3},{4... | collective-permute-start | bytes 3145736 | tf_op jit(solution)/shard_map/ppermute | solution.py:14
  151.1 12.0 %all_gather.3 = f32[32,128]{1,0:T(8,128)S(1)} all-gather(f32[8,128]{1,0:T(8,128)S(1)} %broadcast_multiply_fusion), channel_id=1, replica_groups=mesh['xh'=2,'c'=2,'y'=4,'z'=32,'xl'=2] {'c','xh'}, dimensions={0}, use_global_device_ids=true | all-gather | bytes 20480 | tf_op jit(solution)/shard_map/all_gather | solution.py:90
  163.1 0.6 fusion.10
  163.7 0.0 collective-permute-done.1
  163.7 0.0 copy-done
  163.7 0.5 fusion.2
  164.2 0.6 broadcast_select_fusion
  164.8 0.0 copy-done.3
  164.8 1.8 %convolution_convert_fusion = bf16[128,4096]{1,0:T(8,128)(2,1)} fusion(bf16[4096,128]{1,0:T(8,128)(2,1)S(1)} %collective-permute-done.1, bf16[4096,128]{1,0:T(8,128)(2,1)S(1)} %bitcast.12, bf16[128,128]{1,0:T(8,128)(2,1)S(1)} %copy-done.2, bf16[128,128]{1,0:T(8,128)(2,1)S(1)} %copy-done.3), kind=kOutput, calls=%fused_computation | convolution fusion | flops 273285120 | bytes 3211264 | tf_op jit(solution)/shard_map/dot_general | solution.py:97
  (15 shorter events, 0.2 us)
Async XLA Ops:
  8.2 20.0 %collective-permute-start = (f32[2,4,2,32,8,128]{5,4,3,2,1,0:T(8,128)}, f32[2,4,2,32,8,128]{5,4,3,2,1,0:T(8,128)S(1)}, u32[]{:S(2)}, u32[]{:S(2)}) collective-permute-start(f32[2,4,2,32,8,128]{5,4,3,2,1,0:T(8,128)} %shard_map.92), channel_id=1, source_target_pairs={{0,256},{256,0},{1,257},{257,1},{2,258},{258,2},{3,259},{259,3},{4... | collective-permute-start | bytes 6291464 | tf_op jit(solution)/shard_map/ppermute | solution.py:14
  28.2 1.3 copy-start.1
  36.2 3.9 %copy-start.4 = (bf16[16,128]{1,0:T(8,128)(2,1)S(1)}, bf16[16,128]{1,0:T(8,128)(2,1)}, u32[]{:S(2)}) copy-start(bf16[16,128]{1,0:T(8,128)(2,1)} %param.7) | copy-start | bytes 12292
  36.2 3.9 %copy-start.5 = (bf16[16,128]{1,0:T(8,128)(2,1)S(1)}, bf16[16,128]{1,0:T(8,128)(2,1)}, u32[]{:S(2)}) copy-start(bf16[16,128]{1,0:T(8,128)(2,1)} %param.6) | copy-start | bytes 12292
  36.2 34.4 %all-to-all-start = ((f32[16,32,8,128]{3,2,1,0:T(8,128)}), f32[16,32,8,128]{3,2,1,0:T(8,128)S(1)}, u32[]{:S(2)}, u32[]{:S(2)}) async-start(f32[16,32,8,128]{3,2,1,0:T(8,128)} %bitcast.8), calls=%async_computation | async-start | bytes 4194304 | tf_op jit(solution)/shard_map/all_to_all | solution.py:72
  123.8 39.8 %copy-start = (bf16[128,4096]{1,0:T(8,128)(2,1)S(1)}, bf16[128,4096]{1,0:T(8,128)(2,1)}, u32[]{:S(2)}) copy-start(bf16[128,4096]{1,0:T(8,128)(2,1)} %act_ref.3) | copy-start | bytes 3145732
  145.6 18.1 %collective-permute-start.1 = (bf16[4096,128]{1,0:T(8,128)(2,1)S(1)}, bf16[4096,128]{1,0:T(8,128)(2,1)S(1)}, u32[]{:S(2)}, u32[]{:S(2)}) collective-permute-start(bf16[4096,128]{1,0:T(8,128)(2,1)S(1)} %bitcast.10), channel_id=1, source_target_pairs={{0,256},{256,0},{1,257},{257,1},{2,258},{258,2},{3,259},{259,3},{4... | collective-permute-start | bytes 3145736 | tf_op jit(solution)/shard_map/ppermute | solution.py:14
  163.7 1.1 copy-start.2
  163.7 1.1 copy-start.3

commit v3 on v2

v3 whole, which is shorter than its diff:
```python
import math

import jax
import jax.numpy as jnp
from jax import lax
from jax.experimental import pallas as pl
from jax.experimental.pallas import tpu as pltpu
from jax.sharding import Mesh, PartitionSpec as P

PLANE = ("xh", "y", "xl")
NEAR = ("xh", "y", "zl", "xl")


def swap_cores(block):
    return lax.ppermute(block, "c", [(0, 1), (1, 0)])


def pick(first, second):
    return lax.select(lax.axis_index("c") == 0, first, second)


def exchange(blocks, axes):
    return lax.all_to_all(blocks, axes, 0, 0, tiled=True)


def copies(block, count):
    return jnp.broadcast_to(block[None], (count,) + block.shape)


def terms_kernel(lows, act_ref, cot_ref, *refs):
    out_ref = refs[-1]
    _, ys, _, tiles, half, head = out_ref.shape
    zs = tiles - tiles % 2
    highs = zs // lows
    cut = 2
    span = highs // cut
    block = act_ref.shape[1] // (ys * cut)
    peak = jnp.zeros((half, head), jnp.float32)
    for y in range(ys):
        for z in range(cut):
            start = (y * cut + z) * block
            part = lax.dot_general(
                act_ref[:, start : start + block],
                cot_ref[...],
                (((0,), (0,)), ((), ())),
                preferred_element_type=jnp.float32,
            ).reshape(span, lows, 2, 2, half, head)
            for i in range(2):
                for j in range(2):
                    for low in range(lows):
                        place = low * highs + z * span
                        piece = part[:, low, j, i]
                        if len(refs) == 2:
                            piece = piece + refs[0][i, y, j, place : place + span]
                            peak = jnp.maximum(peak, jnp.abs(piece).max(axis=0))
                        out_ref[i, y, j, place : place + span] = piece
    if len(refs) == 2:
        top = jnp.broadcast_to(jnp.max(peak, keepdims=True), (half, head))
        level = jnp.floor(jnp.log2(32768.0 / jnp.maximum(top, 1e-30)))
        scale = jnp.exp2(level)
        for i in range(2):
            for y in range(ys):
                for j in range(2):
                    out_ref[i, y, j, :zs] = out_ref[i, y, j, :zs] * scale[None]
                    out_ref[i, y, j, zs] = level


def terms(activations, cotangent, *arrived):
    tokens, width = activations.shape
    head = cotangent.shape[1]
    ys, lows = lax.axis_size("y"), lax.axis_size("zl")
    zs = lows * lax.axis_size("zh")
    half = width // (4 * ys * zs)
    return pl.pallas_call(
        lambda *refs: terms_kernel(lows, *refs),
        out_shape=jax.ShapeDtypeStruct((2, ys, 2, zs + len(arrived), half, head), jnp.float32),
        compiler_params=pltpu.CompilerParams(vmem_limit_bytes=40 * 2**20),
        cost_estimate=pl.CostEstimate(
            flops=2 * tokens * width * head, bytes_accessed=6 * width * head, transcendentals=0
        ),
    )(activations, cotangent, *arrived)


def body(activations, w_query, w_key, grad_query, grad_key):
    width = activations.shape[1]
    rows, head = w_query.shape
    ys, highs, lows = (lax.axis_size(a) for a in ("y", "zh", "zl"))
    half = rows // 2
    plane = 4 * ys
    factor = 1.0 / math.sqrt(activations.shape[0] * 2 * plane * highs * lows)

    mine = pick(grad_query, grad_key)
    other = pick(grad_key, grad_query)
    arrived = swap_cores(terms(activations, other))
    sent = terms(activations, mine, arrived).astype(jnp.float16)
    landed = exchange(sent.reshape((plane,) + sent.shape[3:]), PLANE).astype(jnp.float32)
    summed = (landed[:, :-1] * jnp.exp2(-landed[:, -1:])).sum(axis=0)
    summed = exchange(summed.reshape(lows, highs, half, head), "zl").sum(axis=0)

    own = pick(w_query, w_key)
    own = lax.dynamic_slice_in_dim(own, lax.axis_index("xh") * half, half, 0)
    high = lax.reduce_precision(summed, 8, 7)
    parts = [copies(own, highs), high.astype(jnp.bfloat16), (summed - high).astype(jnp.bfloat16)]
    landed = exchange(jnp.concatenate(parts, axis=1), "zh")
    column = landed[:, :half]
    summed = landed[:, half:].astype(jnp.float32)
    summed = (summed[:, :half] + summed[:, half:]).sum(axis=0) * factor

    sheet = exchange(copies(column, plane * lows), NEAR)
    whole = lax.all_gather(summed, ("c", "xh"), axis=0, tiled=True)
    sheet, whole = lax.optimization_barrier((sheet, whole))
    sheet = sheet.reshape(2, ys, lows, 2, highs, half, head).transpose(1, 4, 2, 3, 0, 5, 6)
    sheet = sheet.reshape(width, head)
    other_sheet = swap_cores(sheet)

    weights = jnp.concatenate([sheet, other_sheet], axis=1)
    cotangent = jnp.concatenate([mine, other], axis=1)
    projected = jnp.dot(activations, weights, preferred_element_type=jnp.float32).astype(jnp.bfloat16)
    grad_input = lax.dot_general(
        cotangent, weights, (((1,), (1,)), ((), ())), preferred_element_type=jnp.float32
    ).astype(jnp.bfloat16)
    first, second = projected[:, :head], projected[:, head:]
    return (pick(first, second), pick(second, first), grad_input, whole[:rows], whole[rows:])


def solution(mesh):
    names = ("xh", "c", "y", "zh", "zl", "xl")
    shape = (2, 2, 4, mesh.shape["shard"] // 32, 4, 2)
    fine = Mesh(mesh.devices.reshape(shape), names)
    tokens = P(names, None)
    weights = P(("y", "zh", "zl", "xl"), None)
    return jax.shard_map(
        body,
        mesh=fine,
        in_specs=(tokens, weights, weights, tokens, tokens),
        out_specs=(tokens, tokens, tokens, weights, weights),
        check_vma=False,
    )
```

time: 167 us -> 139 us (0.83)
  waiting for transfers between devices: 34.5 us -> 19.1 us
  Pallas kernels: 12.8 us -> 1.26 us
  blocking collectives: 86.3 us -> 77.9 us
  starting transfers between devices: 25.3 us -> 30.9 us
    all_to_all x1 -> x2, waiting for transfers between devices: 30.5 us -> 13.7 us  [exchange(): return lax.all_to_all(blocks, axes, 0, 0, tiled=True)]
    all_to_all x2, blocking collectives: 74.3 us -> 60.5 us  [exchange(): return lax.all_to_all(blocks, axes, 0, 0, tiled=True)]
    pallas_call x2, Pallas kernels: 12.8 us -> 1.26 us  [terms(): pl.pallas_call(lambda *refs: terms_kernel(lows, *refs), out_shape=jax.Sha...]
    all_to_all x1 -> x2, starting transfers between devices: 3.85 us -> 9.74 us  [exchange(): return lax.all_to_all(blocks, axes, 0, 0, tiled=True)]
    all_gather x1, blocking collectives: 12 us -> 17.4 us  [body(): whole = lax.all_gather(summed, ('c', 'xh'), axis=0, tiled=True)]
  transfers between devices with their start and end apart: 3 -> 4, of which waited for: 2 -> 4; matrix products, arithmetic and copies ran while one was open for 0% -> 0% of each run, Pallas kernels for 0% -> 0%
where the time goes in v3:
time: 139 us; the launch traced here: 138 us
  blocking collectives  77.9 us (56%)
  starting transfers between devices  30.9 us (22%)
  waiting for transfers between devices  19.1 us (14%)
  local copies, waits for them, and re-layouts  3.35 us (2%)
  other arithmetic  2.59 us (2%)
  matrix products  2.26 us (2%)
    all_to_all x2, blocking collectives, exchange(): return lax.all_to_all(blocks, axes, 0, 0, tiled=True)  60.5 us
    ppermute x2, starting transfers between devices, swap_cores(): return lax.ppermute(block, 'c', [(0, 1), (1, 0)])  21.2 us
    all_gather x1, blocking collectives, body(): whole = lax.all_gather(summed, ('c', 'xh'), axis=0, tiled=True)  17.4 us
    all_to_all x2, waiting for transfers between devices, exchange(): return lax.all_to_all(blocks, axes, 0, 0, tiled=True)  13.7 us
    all_to_all x2, starting transfers between devices, exchange(): return lax.all_to_all(blocks, axes, 0, 0, tiled=True)  9.74 us
    ppermute x2, waiting for transfers between devices, swap_cores(): return lax.ppermute(block, 'c', [(0, 1), (1, 0)])  5.42 us
  transfers between devices with their start and end apart: 4, of which 4 were waited for; matrix products, arithmetic and copies ran while one was open for 0% of the time, Pallas kernels for 0%

profile of v3, /device:TPU:1, one launch (start us, length us, event | category | flops | bytes accessed | tf_op | source)
XLA Modules:
  0.0 138.2 jit_solution(5088840432212967855)
XLA Ops:
  0.6 0.8 broadcast_select_fusion.2
  1.4 1.2 copy-done
  2.6 0.5 shard_map.92
  3.1 16.1 %collective-permute-start = (f32[2,4,2,32,8,128]{5,4,3,2,1,0:T(8,128)S(1)}, f32[2,4,2,32,8,128]{5,4,3,2,1,0:T(8,128)S(1)}, u32[]{:S(2)}, u32[]{:S(2)}) collective-permute-start(f32[2,4,2,32,8,128]{5,4,3,2,1,0:T(8,128)S(1)} %shard_map.92), channel_id=1, source_target_pairs={{0,256},{256,0},{1,257},{257,1},{2,258},{258,2},{3,259},{259,3},{4... | collective-permute-start | bytes 6291464 | tf_op jit(solution)/shard_map/ppermute | solution.py:15
  19.2 3.8 %collective-permute-done.refs_2_ = f32[2,4,2,32,8,128]{5,4,3,2,1,0:T(8,128)S(1)} collective-permute-done((f32[2,4,2,32,8,128]{5,4,3,2,1,0:T(8,128)S(1)}, f32[2,4,2,32,8,128]{5,4,3,2,1,0:T(8,128)S(1)}, u32[]{:S(2)}, u32[]{:S(2)}) %collective-permute-start) | collective-permute-done | bytes 2097184 | tf_op jit(solution)/shard_map/ppermute | solution.py:15
  23.0 0.8 shard_map.93
  23.8 0.1 convert_element_type.24
  23.9 19.8 %all_to_all.20 = f16[16,33,8,128]{3,2,1,0:T(8,128)(2,1)S(1)} all-to-all(f16[16,33,8,128]{3,2,1,0:T(8,128)(2,1)S(1)} %bitcast.11), channel_id=1, replica_groups=mesh['xh'=2,'c'=2,'y'=4,'zh'=8,'zl'=4,'xl'=2] {'xh','y','xl'}, dimensions={0} | all-to-all | bytes 2162688 | tf_op jit(solution)/shard_map/all_to_all | solution.py:23
  43.7 0.1 convert_element_type.25
  43.9 0.8 fusion
  44.7 3.3 %all-to-all-start.1 = ((f32[4,8,8,128]{3,2,1,0:T(8,128)}), f32[4,8,8,128]{3,2,1,0:T(8,128)S(1)}, u32[]{:S(2)}, u32[]{:S(2)}) async-start(f32[4,8,8,128]{3,2,1,0:T(8,128)} %bitcast.2), calls=%async_computation.1 | async-start | bytes 262144 | tf_op jit(solution)/shard_map/all_to_all | solution.py:23
  48.1 4.7 %all-to-all-done.1 = f32[4,8,8,128]{3,2,1,0:T(8,128)S(1)} async-done(((f32[4,8,8,128]{3,2,1,0:T(8,128)}), f32[4,8,8,128]{3,2,1,0:T(8,128)S(1)}, u32[]{:S(2)}, u32[]{:S(2)}) %all-to-all-start.1) | async-done | bytes 131104 | tf_op jit(solution)/shard_map/all_to_all | solution.py:23
  52.8 40.7 %all_to_all.21 = bf16[8,24,128]{2,1,0:T(8,128)(2,1)S(1)} all-to-all(bf16[8,24,128]{2,1,0:T(8,128)(2,1)S(1)} %pad_maximum_fusion.7), channel_id=1, replica_groups=mesh['xh'=2,'c'=2,'y'=4,'zh'=8,'zl'=4,'xl'=2] {'zh'}, dimensions={0} | all-to-all | bytes 98304 | tf_op jit(solution)/shard_map/all_to_all | solution.py:23
  93.6 1.2 broadcast_in_dim.5
  94.8 6.4 %all-to-all-start.3 = ((bf16[64,8,8,128]{3,2,1,0:T(8,128)(2,1)}), bf16[64,8,8,128]{3,2,1,0:T(8,128)(2,1)S(1)}, u32[]{:S(2)}, u32[]{:S(2)}) async-start(bf16[64,8,8,128]{3,2,1,0:T(8,128)(2,1)} %broadcast_in_dim.5), calls=%async_computation.3 | async-start | bytes 2097152 | tf_op jit(solution)/shard_map/all_to_all | solution.py:23
  101.3 17.4 %all_gather.3 = f32[32,128]{1,0:T(8,128)S(1)} all-gather(f32[8,128]{1,0:T(8,128)S(1)} %broadcast_multiply_fusion), channel_id=1, replica_groups=mesh['xh'=2,'c'=2,'y'=4,'zh'=8,'zl'=4,'xl'=2] {'c','xh'}, dimensions={0}, use_global_device_ids=true | all-gather | bytes 20480 | tf_op jit(solution)/shard_map/all_gather | solution.py:110
  118.7 9.0 %all-to-all-done.3 = bf16[64,8,8,128]{3,2,1,0:T(8,128)(2,1)S(1)} async-done(((bf16[64,8,8,128]{3,2,1,0:T(8,128)(2,1)}), bf16[64,8,8,128]{3,2,1,0:T(8,128)(2,1)S(1)}, u32[]{:S(2)}, u32[]{:S(2)}) %all-to-all-start.3) | async-done | bytes 1048608 | tf_op jit(solution)/shard_map/all_to_all | solution.py:23
  127.6 0.3 copy.14
  127.9 5.1 %collective-permute-start.1 = (bf16[4096,128]{1,0:T(8,128)(2,1)S(1)}, bf16[4096,128]{1,0:T(8,128)(2,1)S(1)}, u32[]{:S(2)}, u32[]{:S(2)}) collective-permute-start(bf16[4096,128]{1,0:T(8,128)(2,1)S(1)} %bitcast.13), channel_id=1, source_target_pairs={{0,256},{256,0},{1,257},{257,1},{2,258},{258,2},{3,259},{259,3},{4... | collective-permute-start | bytes 3145736 | tf_op jit(solution)/shard_map/ppermute | solution.py:15
  133.0 0.6 fusion.14
  133.7 1.7 %collective-permute-done.1 = bf16[4096,128]{1,0:T(8,128)(2,1)S(1)} collective-permute-done((bf16[4096,128]{1,0:T(8,128)(2,1)S(1)}, bf16[4096,128]{1,0:T(8,128)(2,1)S(1)}, u32[]{:S(2)}, u32[]{:S(2)}) %collective-permute-start.1) | collective-permute-done | bytes 1048608 | tf_op jit(solution)/shard_map/ppermute | solution.py:15
  135.3 0.5 fusion.3
  135.8 0.6 broadcast_select_fusion
  136.4 1.8 %convolution_convert_fusion = bf16[128,4096]{1,0:T(8,128)(2,1)} fusion(bf16[4096,128]{1,0:T(8,128)(2,1)S(1)} %collective-permute-done.1, bf16[4096,128]{1,0:T(8,128)(2,1)S(1)} %bitcast.15, bf16[128,128]{1,0:T(8,128)(2,1)S(1)} %get-tuple-element.11.refs_1_, bf16[128,128]{1,0:T(8,128)(2,1)S(1)} %get-tuple-element.12.refs_1_), kind=kOutput, calls=%fused_computation | convolution fusion | flops 273285120 | bytes 3211264 | tf_op jit(solution)/shard_map/dot_general | solution.py:119
  (17 shorter events, 0.1 us)
Async XLA Ops:
  1.4 1.2 copy-start
  3.1 19.8 %collective-permute-start = (f32[2,4,2,32,8,128]{5,4,3,2,1,0:T(8,128)S(1)}, f32[2,4,2,32,8,128]{5,4,3,2,1,0:T(8,128)S(1)}, u32[]{:S(2)}, u32[]{:S(2)}) collective-permute-start(f32[2,4,2,32,8,128]{5,4,3,2,1,0:T(8,128)S(1)} %shard_map.92), channel_id=1, source_target_pairs={{0,256},{256,0},{1,257},{257,1},{2,258},{258,2},{3,259},{259,3},{4... | collective-permute-start | bytes 6291464 | tf_op jit(solution)/shard_map/ppermute | solution.py:15
  43.8 4.2 %copy-start.2 = (bf16[16,128]{1,0:T(8,128)(2,1)S(1)}, bf16[16,128]{1,0:T(8,128)(2,1)}, u32[]{:S(2)}) copy-start(bf16[16,128]{1,0:T(8,128)(2,1)} %param.7) | copy-start | bytes 12292
  43.8 4.2 %copy-start.3 = (bf16[16,128]{1,0:T(8,128)(2,1)S(1)}, bf16[16,128]{1,0:T(8,128)(2,1)}, u32[]{:S(2)}) copy-start(bf16[16,128]{1,0:T(8,128)(2,1)} %param.6) | copy-start | bytes 12292
  44.7 8.1 %all-to-all-start.1 = ((f32[4,8,8,128]{3,2,1,0:T(8,128)}), f32[4,8,8,128]{3,2,1,0:T(8,128)S(1)}, u32[]{:S(2)}, u32[]{:S(2)}) async-start(f32[4,8,8,128]{3,2,1,0:T(8,128)} %bitcast.2), calls=%async_computation.1 | async-start | bytes 262144 | tf_op jit(solution)/shard_map/all_to_all | solution.py:23
  94.8 40.5 %copy-start.1 = (bf16[128,4096]{1,0:T(8,128)(2,1)S(1)}, bf16[128,4096]{1,0:T(8,128)(2,1)}, u32[]{:S(2)}) copy-start(bf16[128,4096]{1,0:T(8,128)(2,1)} %refs_0_.3) | copy-start | bytes 3145732
  94.8 32.8 %all-to-all-start.3 = ((bf16[64,8,8,128]{3,2,1,0:T(8,128)(2,1)}), bf16[64,8,8,128]{3,2,1,0:T(8,128)(2,1)S(1)}, u32[]{:S(2)}, u32[]{:S(2)}) async-start(bf16[64,8,8,128]{3,2,1,0:T(8,128)(2,1)} %broadcast_in_dim.5), calls=%async_computation.3 | async-start | bytes 2097152 | tf_op jit(solution)/shard_map/all_to_all | solution.py:23
  127.9 7.4 %collective-permute-start.1 = (bf16[4096,128]{1,0:T(8,128)(2,1)S(1)}, bf16[4096,128]{1,0:T(8,128)(2,1)S(1)}, u32[]{:S(2)}, u32[]{:S(2)}) collective-permute-start(bf16[4096,128]{1,0:T(8,128)(2,1)S(1)} %bitcast.13), channel_id=1, source_target_pairs={{0,256},{256,0},{1,257},{257,1},{2,258},{258,2},{3,259},{259,3},{4... | collective-permute-start | bytes 3145736 | tf_op jit(solution)/shard_map/ppermute | solution.py:15

commit v4 on v3

--- a/solution.py
+++ b/solution.py
@@ -7,8 +7,7 @@
 from jax.experimental.pallas import tpu as pltpu
 from jax.sharding import Mesh, PartitionSpec as P
 
-PLANE = ("xh", "y", "xl")
-NEAR = ("xh", "y", "zl", "xl")
+NEAR = ("xh", "y", "xl", "zl")
 
 
 def swap_cores(block):
@@ -27,11 +26,9 @@
     return jnp.broadcast_to(block[None], (count,) + block.shape)
 
 
-def terms_kernel(lows, act_ref, cot_ref, *refs):
+def terms_kernel(highs, act_ref, cot_ref, *refs):
     out_ref = refs[-1]
-    _, ys, _, tiles, half, head = out_ref.shape
-    zs = tiles - tiles % 2
-    highs = zs // lows
+    _, ys, _, lows, _, half, head = out_ref.shape
     cut = 2
     span = highs // cut
     block = act_ref.shape[1] // (ys * cut)
@@ -48,12 +45,11 @@
             for i in range(2):
                 for j in range(2):
                     for low in range(lows):
-                        place = low * highs + z * span
                         piece = part[:, low, j, i]
                         if len(refs) == 2:
-                            piece = piece + refs[0][i, y, j, place : place + span]
+                            piece = piece + refs[0][i, y, j, low, z * span : (z + 1) * span]
                             peak = jnp.maximum(peak, jnp.abs(piece).max(axis=0))
-                        out_ref[i, y, j, place : place + span] = piece
+                        out_ref[i, y, j, low, z * span : (z + 1) * span] = piece
     if len(refs) == 2:
         top = jnp.broadcast_to(jnp.max(peak, keepdims=True), (half, head))
         level = jnp.floor(jnp.log2(32768.0 / jnp.maximum(top, 1e-30)))
@@ -61,19 +57,21 @@
         for i in range(2):
             for y in range(ys):
                 for j in range(2):
-                    out_ref[i, y, j, :zs] = out_ref[i, y, j, :zs] * scale[None]
-                    out_ref[i, y, j, zs] = level
+                    for low in range(lows):
+                        out_ref[i, y, j, low, :highs] = out_ref[i, y, j, low, :highs] * scale[None]
+                        out_ref[i, y, j, low, highs] = level
 
 
 def terms(activations, cotangent, *arrived):
     tokens, width = activations.shape
     head = cotangent.shape[1]
-    ys, lows = lax.axis_size("y"), lax.axis_size("zl")
-    zs = lows * lax.axis_size("zh")
-    half = width // (4 * ys * zs)
+    ys, lows, highs = (lax.axis_size(a) for a in ("y", "zl", "zh"))
+    half = width // (4 * ys * lows * highs)
     return pl.pallas_call(
-        lambda *refs: terms_kernel(lows, *refs),
-        out_shape=jax.ShapeDtypeStruct((2, ys, 2, zs + len(arrived), half, head), jnp.float32),
+        lambda *refs: terms_kernel(highs, *refs),
+        out_shape=jax.ShapeDtypeStruct(
+            (2, ys, 2, lows, highs + len(arrived), half, head), jnp.float32
+        ),
         compiler_params=pltpu.CompilerParams(vmem_limit_bytes=40 * 2**20),
         cost_estimate=pl.CostEstimate(
             flops=2 * tokens * width * head, bytes_accessed=6 * width * head, transcendentals=0
@@ -86,16 +84,15 @@
     rows, head = w_query.shape
     ys, highs, lows = (lax.axis_size(a) for a in ("y", "zh", "zl"))
     half = rows // 2
-    plane = 4 * ys
-    factor = 1.0 / math.sqrt(activations.shape[0] * 2 * plane * highs * lows)
+    near = 4 * ys * lows
+    factor = 1.0 / math.sqrt(activations.shape[0] * 2 * near * highs)
 
     mine = pick(grad_query, grad_key)
     other = pick(grad_key, grad_query)
     arrived = swap_cores(terms(activations, other))
     sent = terms(activations, mine, arrived).astype(jnp.float16)
-    landed = exchange(sent.reshape((plane,) + sent.shape[3:]), PLANE).astype(jnp.float32)
+    landed = exchange(sent.reshape((near,) + sent.shape[4:]), NEAR).astype(jnp.float32)
     summed = (landed[:, :-1] * jnp.exp2(-landed[:, -1:])).sum(axis=0)
-    summed = exchange(summed.reshape(lows, highs, half, head), "zl").sum(axis=0)
 
     own = pick(w_query, w_key)
     own = lax.dynamic_slice_in_dim(own, lax.axis_index("xh") * half, half, 0)
@@ -106,10 +103,10 @@
     summed = landed[:, half:].astype(jnp.float32)
     summed = (summed[:, :half] + summed[:, half:]).sum(axis=0) * factor
 
-    sheet = exchange(copies(column, plane * lows), NEAR)
+    sheet = exchange(copies(column, near), NEAR)
     whole = lax.all_gather(summed, ("c", "xh"), axis=0, tiled=True)
     sheet, whole = lax.optimization_barrier((sheet, whole))
-    sheet = sheet.reshape(2, ys, lows, 2, highs, half, head).transpose(1, 4, 2, 3, 0, 5, 6)
+    sheet = sheet.reshape(2, ys, 2, lows, highs, half, head).transpose(1, 4, 3, 2, 0, 5, 6)
     sheet = sheet.reshape(width, head)
     other_sheet = swap_cores(sheet)
 
@@ -125,7 +122,7 @@
 
 def solution(mesh):
     names = ("xh", "c", "y", "zh", "zl", "xl")
-    shape = (2, 2, 4, mesh.shape["shard"] // 32, 4, 2)
+    shape = (2, 2, 4, mesh.shape["shard"] // 16, 2, 2)
     fine = Mesh(mesh.devices.reshape(shape), names)
     tokens = P(names, None)
     weights = P(("y", "zh", "zl", "xl"), None)

time: 139 us -> 126 us (0.906)
  blocking collectives: 77.9 us -> 64.2 us
  waiting for transfers between devices: 19.1 us -> 23.6 us
  starting transfers between devices: 30.9 us -> 26.7 us
    all_to_all x2 -> x1, blocking collectives: 60.5 us -> 42.7 us  [exchange(): return lax.all_to_all(blocks, axes, 0, 0, tiled=True)]
    all_to_all x2, waiting for transfers between devices: 13.7 us -> 18.2 us  [exchange(): return lax.all_to_all(blocks, axes, 0, 0, tiled=True)]
    all_gather x1, blocking collectives: 17.4 us -> 21.6 us  [body(): whole = lax.all_gather(summed, ('c', 'xh'), axis=0, tiled=True)]
    ppermute x2, starting transfers between devices: 21.2 us -> 18.7 us  [swap_cores(): return lax.ppermute(block, 'c', [(0, 1), (1, 0)])]
    all_to_all x2, starting transfers between devices: 9.74 us -> 8 us  [exchange(): return lax.all_to_all(blocks, axes, 0, 0, tiled=True)]
  transfers between devices with their start and end apart: 4 -> 4, of which waited for: 4 -> 3; matrix products, arithmetic and copies ran while one was open for 0% -> 1% of each run, Pallas kernels for 0% -> 0%
where the time goes in v4:
time: 126 us; the launch traced here: 125 us
  blocking collectives  64.2 us (51%)
  starting transfers between devices  26.7 us (21%)
  waiting for transfers between devices  23.6 us (19%)
  local copies, waits for them, and re-layouts  3.35 us (3%)
  other arithmetic  3.03 us (2%)
  matrix products  2.26 us (2%)
  Pallas kernels  1.29 us (1%)
    all_to_all x1, blocking collectives, exchange(): return lax.all_to_all(blocks, axes, 0, 0, tiled=True)  42.7 us
    all_gather x1, blocking collectives, body(): whole = lax.all_gather(summed, ('c', 'xh'), axis=0, tiled=True)  21.6 us
    ppermute x2, starting transfers between devices, swap_cores(): return lax.ppermute(block, 'c', [(0, 1), (1, 0)])  18.7 us
    all_to_all x2, waiting for transfers between devices, exchange(): return lax.all_to_all(blocks, axes, 0, 0, tiled=True)  18.2 us
    all_to_all x2, starting transfers between devices, exchange(): return lax.all_to_all(blocks, axes, 0, 0, tiled=True)  8 us
    ppermute x2, waiting for transfers between devices, swap_cores(): return lax.ppermute(block, 'c', [(0, 1), (1, 0)])  5.42 us
  transfers between devices with their start and end apart: 4, of which 3 were waited for; matrix products, arithmetic and copies ran while one was open for 1% of the time, Pallas kernels for 0%

profile of v4, /device:TPU:1, one launch (start us, length us, event | category | flops | bytes accessed | tf_op | source)
XLA Modules:
  0.0 125.2 jit_solution(4253232142066385159)
XLA Ops:
  0.6 0.8 broadcast_select_fusion.2
  1.4 1.2 copy-done
  2.6 0.5 shard_map.92
  3.1 16.1 %collective-permute-start = (f32[2,4,2,2,16,8,128]{6,5,4,3,2,1,0:T(8,128)S(1)}, f32[2,4,2,2,16,8,128]{6,5,4,3,2,1,0:T(8,128)S(1)}, u32[]{:S(2)}, u32[]{:S(2)}) collective-permute-start(f32[2,4,2,2,16,8,128]{6,5,4,3,2,1,0:T(8,128)S(1)} %shard_map.92), channel_id=1, source_target_pairs={{0,256},{256,0},{1,257},{257,1},{2,258},{258,2},{3,259},{259,3},{4... | collective-permute-start | bytes 6291464 | tf_op jit(solution)/shard_map/ppermute | solution.py:14
  19.2 3.8 %collective-permute-done.refs_2_ = f32[2,4,2,2,16,8,128]{6,5,4,3,2,1,0:T(8,128)S(1)} collective-permute-done((f32[2,4,2,2,16,8,128]{6,5,4,3,2,1,0:T(8,128)S(1)}, f32[2,4,2,2,16,8,128]{6,5,4,3,2,1,0:T(8,128)S(1)}, u32[]{:S(2)}, u32[]{:S(2)}) %collective-permute-start) | collective-permute-done | bytes 2097184 | tf_op jit(solution)/shard_map/ppermute | solution.py:14
  23.0 0.8 shard_map.93
  23.8 0.0 copy-start.2
  23.8 0.0 copy-start.3
  23.8 1.1 convert_element_type.24
  25.0 3.9 %all-to-all-start = ((f16[32,17,8,128]{3,2,1,0:T(8,128)(2,1)}), f16[32,17,8,128]{3,2,1,0:T(8,128)(2,1)S(1)}, u32[]{:S(2)}, u32[]{:S(2)}) async-start(f16[32,17,8,128]{3,2,1,0:T(8,128)(2,1)} %bitcast), calls=%async_computation | async-start | bytes 2228224 | tf_op jit(solution)/shard_map/all_to_all | solution.py:22
  29.0 18.2 %all-to-all-done = f16[32,17,8,128]{3,2,1,0:T(8,128)(2,1)S(1)} async-done(((f16[32,17,8,128]{3,2,1,0:T(8,128)(2,1)}), f16[32,17,8,128]{3,2,1,0:T(8,128)(2,1)S(1)}, u32[]{:S(2)}, u32[]{:S(2)}) %all-to-all-start) | async-done | bytes 1114144 | tf_op jit(solution)/shard_map/all_to_all | solution.py:22
  47.1 0.1 convert_element_type.25
  47.3 0.2 fusion
  47.6 42.7 %all_to_all.15 = bf16[16,24,128]{2,1,0:T(8,128)(2,1)S(1)} all-to-all(bf16[16,24,128]{2,1,0:T(8,128)(2,1)S(1)} %pad_maximum_fusion.7), channel_id=1, replica_groups=mesh['xh'=2,'c'=2,'y'=4,'zh'=16,'zl'=2,'xl'=2] {'zh'}, dimensions={0} | all-to-all | bytes 196608 | tf_op jit(solution)/shard_map/all_to_all | solution.py:22
  90.3 1.2 broadcast_in_dim.5
  91.5 4.1 %all-to-all-start.2 = ((bf16[32,16,8,128]{3,2,1,0:T(8,128)(2,1)}), bf16[32,16,8,128]{3,2,1,0:T(8,128)(2,1)S(1)}, u32[]{:S(2)}, u32[]{:S(2)}) async-start(bf16[32,16,8,128]{3,2,1,0:T(8,128)(2,1)} %broadcast_in_dim.5), calls=%async_computation.2 | async-start | bytes 2097152 | tf_op jit(solution)/shard_map/all_to_all | solution.py:22
  95.6 21.6 %all_gather.3 = f32[32,128]{1,0:T(8,128)S(1)} all-gather(f32[8,128]{1,0:T(8,128)S(1)} %broadcast_multiply_fusion), channel_id=1, replica_groups=mesh['xh'=2,'c'=2,'y'=4,'zh'=16,'zl'=2,'xl'=2] {'c','xh'}, dimensions={0}, use_global_device_ids=true | all-gather | bytes 20480 | tf_op jit(solution)/shard_map/all_gather | solution.py:107
  117.2 0.3 copy.12
  117.5 2.6 %collective-permute-start.1 = (bf16[4096,128]{1,0:T(8,128)(2,1)S(1)}, bf16[4096,128]{1,0:T(8,128)(2,1)S(1)}, u32[]{:S(2)}, u32[]{:S(2)}) collective-permute-start(bf16[4096,128]{1,0:T(8,128)(2,1)S(1)} %bitcast.11), channel_id=1, source_target_pairs={{0,256},{256,0},{1,257},{257,1},{2,258},{258,2},{3,259},{259,3},{4... | collective-permute-start | bytes 3145736 | tf_op jit(solution)/shard_map/ppermute | solution.py:14
  120.1 0.6 fusion.14
  120.7 1.7 %collective-permute-done.1 = bf16[4096,128]{1,0:T(8,128)(2,1)S(1)} collective-permute-done((bf16[4096,128]{1,0:T(8,128)(2,1)S(1)}, bf16[4096,128]{1,0:T(8,128)(2,1)S(1)}, u32[]{:S(2)}, u32[]{:S(2)}) %collective-permute-start.1) | collective-permute-done | bytes 1048608 | tf_op jit(solution)/shard_map/ppermute | solution.py:14
  122.3 0.5 fusion.3
  122.8 0.6 broadcast_select_fusion
  123.5 1.8 %convolution_convert_fusion = bf16[128,4096]{1,0:T(8,128)(2,1)} fusion(bf16[4096,128]{1,0:T(8,128)(2,1)S(1)} %collective-permute-done.1, bf16[4096,128]{1,0:T(8,128)(2,1)S(1)} %bitcast.13, bf16[128,128]{1,0:T(8,128)(2,1)S(1)} %get-tuple-element.13.refs_1_, bf16[128,128]{1,0:T(8,128)(2,1)S(1)} %get-tuple-element.14.refs_1_), kind=kOutput, calls=%fused_computation | convolution fusion | flops 273285120 | bytes 3211264 | tf_op jit(solution)/shard_map/dot_general | solution.py:116
  (15 shorter events, 0.1 us)
Async XLA Ops:
  1.4 1.2 copy-start
  3.1 19.8 %collective-permute-start = (f32[2,4,2,2,16,8,128]{6,5,4,3,2,1,0:T(8,128)S(1)}, f32[2,4,2,2,16,8,128]{6,5,4,3,2,1,0:T(8,128)S(1)}, u32[]{:S(2)}, u32[]{:S(2)}) collective-permute-start(f32[2,4,2,2,16,8,128]{6,5,4,3,2,1,0:T(8,128)S(1)} %shard_map.92), channel_id=1, source_target_pairs={{0,256},{256,0},{1,257},{257,1},{2,258},{258,2},{3,259},{259,3},{4... | collective-permute-start | bytes 6291464 | tf_op jit(solution)/shard_map/ppermute | solution.py:14
  23.8 5.1 %copy-start.2 = (bf16[16,128]{1,0:T(8,128)(2,1)S(1)}, bf16[16,128]{1,0:T(8,128)(2,1)}, u32[]{:S(2)}) copy-start(bf16[16,128]{1,0:T(8,128)(2,1)} %param.7) | copy-start | bytes 12292
  23.8 5.1 %copy-start.3 = (bf16[16,128]{1,0:T(8,128)(2,1)S(1)}, bf16[16,128]{1,0:T(8,128)(2,1)}, u32[]{:S(2)}) copy-start(bf16[16,128]{1,0:T(8,128)(2,1)} %param.6) | copy-start | bytes 12292
  25.0 22.2 %all-to-all-start = ((f16[32,17,8,128]{3,2,1,0:T(8,128)(2,1)}), f16[32,17,8,128]{3,2,1,0:T(8,128)(2,1)S(1)}, u32[]{:S(2)}, u32[]{:S(2)}) async-start(f16[32,17,8,128]{3,2,1,0:T(8,128)(2,1)} %bitcast), calls=%async_computation | async-start | bytes 2228224 | tf_op jit(solution)/shard_map/all_to_all | solution.py:22
  91.5 30.9 %copy-start.1 = (bf16[128,4096]{1,0:T(8,128)(2,1)S(1)}, bf16[128,4096]{1,0:T(8,128)(2,1)}, u32[]{:S(2)}) copy-start(bf16[128,4096]{1,0:T(8,128)(2,1)} %refs_0_.3) | copy-start | bytes 3145732
  91.5 25.7 %all-to-all-start.2 = ((bf16[32,16,8,128]{3,2,1,0:T(8,128)(2,1)}), bf16[32,16,8,128]{3,2,1,0:T(8,128)(2,1)S(1)}, u32[]{:S(2)}, u32[]{:S(2)}) async-start(bf16[32,16,8,128]{3,2,1,0:T(8,128)(2,1)} %broadcast_in_dim.5), calls=%async_computation.2 | async-start | bytes 2097152 | tf_op jit(solution)/shard_map/all_to_all | solution.py:22
  117.5 4.9 %collective-permute-start.1 = (bf16[4096,128]{1,0:T(8,128)(2,1)S(1)}, bf16[4096,128]{1,0:T(8,128)(2,1)S(1)}, u32[]{:S(2)}, u32[]{:S(2)}) collective-permute-start(bf16[4096,128]{1,0:T(8,128)(2,1)S(1)} %bitcast.11), channel_id=1, source_target_pairs={{0,256},{256,0},{1,257},{257,1},{2,258},{258,2},{3,259},{259,3},{4... | collective-permute-start | bytes 3145736 | tf_op jit(solution)/shard_map/ppermute | solution.py:14

commit v5 on v4

--- a/solution.py
+++ b/solution.py
@@ -10,8 +10,13 @@
 NEAR = ("xh", "y", "xl", "zl")
 
 
-def swap_cores(block):
-    return lax.ppermute(block, "c", [(0, 1), (1, 0)])
+def swap(block, axis):
+    return lax.ppermute(block, axis, [(0, 1), (1, 0)])
+
+
+def ordered(own, came, axis):
+    first = lax.axis_index(axis) == 0
+    return lax.select(first, own, came), lax.select(first, came, own)
 
 
 def pick(first, second):
@@ -89,7 +94,7 @@
 
     mine = pick(grad_query, grad_key)
     other = pick(grad_key, grad_query)
-    arrived = swap_cores(terms(activations, other))
+    arrived = swap(terms(activations, other), "c")
     sent = terms(activations, mine, arrived).astype(jnp.float16)
     landed = exchange(sent.reshape((near,) + sent.shape[4:]), NEAR).astype(jnp.float32)
     summed = (landed[:, :-1] * jnp.exp2(-landed[:, -1:])).sum(axis=0)
@@ -104,11 +109,12 @@
     summed = (summed[:, :half] + summed[:, half:]).sum(axis=0) * factor
 
     sheet = exchange(copies(column, near), NEAR)
-    whole = lax.all_gather(summed, ("c", "xh"), axis=0, tiled=True)
+    both = jnp.stack(ordered(summed, swap(summed, "c"), "c"))
+    whole = jnp.concatenate(ordered(both, swap(both, "xh"), "xh"), axis=1)
     sheet, whole = lax.optimization_barrier((sheet, whole))
     sheet = sheet.reshape(2, ys, 2, lows, highs, half, head).transpose(1, 4, 3, 2, 0, 5, 6)
     sheet = sheet.reshape(width, head)
-    other_sheet = swap_cores(sheet)
+    other_sheet = swap(sheet, "c")
 
     weights = jnp.concatenate([sheet, other_sheet], axis=1)
     cotangent = jnp.concatenate([mine, other], axis=1)
@@ -117,7 +123,7 @@
         cotangent, weights, (((1,), (1,)), ((), ())), preferred_element_type=jnp.float32
     ).astype(jnp.bfloat16)
     first, second = projected[:, :head], projected[:, head:]
-    return (pick(first, second), pick(second, first), grad_input, whole[:rows], whole[rows:])
+    return (pick(first, second), pick(second, first), grad_input, whole[0], whole[1])
 
 
 def solution(mesh):

time: 126 us -> 122 us (0.968)
  blocking collectives: 64.2 us -> 42.7 us
  starting transfers between devices: 26.7 us -> 39.9 us
  waiting for transfers between devices: 23.6 us -> 28.4 us
    all_gather x1 -> x0, blocking collectives: 21.6 us -> none  [body(): whole = lax.all_gather(summed, ('c', 'xh'), axis=0, tiled=True)]
    ppermute x2 -> x4, starting transfers between devices: 18.7 us -> 31.9 us  [swap(): return lax.ppermute(block, axis, [(0, 1), (1, 0)])]
    ppermute x2 -> x4, waiting for transfers between devices: 5.42 us -> 7.92 us  [swap(): return lax.ppermute(block, axis, [(0, 1), (1, 0)])]
    all_to_all x2, waiting for transfers between devices: 18.2 us -> 20.5 us  [exchange(): return lax.all_to_all(blocks, axes, 0, 0, tiled=True)]
  transfers between devices with their start and end apart: 4 -> 6, of which waited for: 3 -> 6; matrix products, arithmetic and copies ran while one was open for 1% -> 1% of each run, Pallas kernels for 0% -> 0%
where the time goes in v5:
time: 122 us
  blocking collectives  42.7 us (35%)
  starting transfers between devices  39.9 us (33%)
  waiting for transfers between devices  28.4 us (23%)
  local copies, waits for them, and re-layouts  3.35 us (3%)
  other arithmetic  3.05 us (2%)
  matrix products  2.26 us (2%)
  Pallas kernels  1.29 us (1%)
    all_to_all x1, blocking collectives, exchange(): return lax.all_to_all(blocks, axes, 0, 0, tiled=True)  42.7 us
    ppermute x4, starting transfers between devices, swap(): return lax.ppermute(block, axis, [(0, 1), (1, 0)])  31.9 us
    all_to_all x2, waiting for transfers between devices, exchange(): return lax.all_to_all(blocks, axes, 0, 0, tiled=True)  20.5 us
    all_to_all x2, starting transfers between devices, exchange(): return lax.all_to_all(blocks, axes, 0, 0, tiled=True)  8 us
    ppermute x4, waiting for transfers between devices, swap(): return lax.ppermute(block, axis, [(0, 1), (1, 0)])  7.92 us
  transfers between devices with their start and end apart: 6, of which 6 were waited for; matrix products, arithmetic and copies ran while one was open for 1% of the time, Pallas kernels for 0%

profile of v5, /device:TPU:1, one launch (start us, length us, event | category | flops | bytes accessed | tf_op | source)
XLA Modules:
  0.0 121.8 jit_solution(2021535146537448418)
XLA Ops:
  0.6 0.8 broadcast_select_fusion.2
  1.4 1.2 copy-done
  2.6 0.5 shard_map.92
  3.1 16.1 %collective-permute-start = (f32[2,4,2,2,16,8,128]{6,5,4,3,2,1,0:T(8,128)S(1)}, f32[2,4,2,2,16,8,128]{6,5,4,3,2,1,0:T(8,128)S(1)}, u32[]{:S(2)}, u32[]{:S(2)}) collective-permute-start(f32[2,4,2,2,16,8,128]{6,5,4,3,2,1,0:T(8,128)S(1)} %shard_map.92), channel_id=1, source_target_pairs={{0,256},{256,0},{1,257},{257,1},{2,258},{258,2},{3,259},{259,3},{4... | collective-permute-start | bytes 6291464 | tf_op jit(solution)/shard_map/ppermute | solution.py:14
  19.2 3.8 %collective-permute-done.refs_2_ = f32[2,4,2,2,16,8,128]{6,5,4,3,2,1,0:T(8,128)S(1)} collective-permute-done((f32[2,4,2,2,16,8,128]{6,5,4,3,2,1,0:T(8,128)S(1)}, f32[2,4,2,2,16,8,128]{6,5,4,3,2,1,0:T(8,128)S(1)}, u32[]{:S(2)}, u32[]{:S(2)}) %collective-permute-start) | collective-permute-done | bytes 2097184 | tf_op jit(solution)/shard_map/ppermute | solution.py:14
  23.0 0.8 shard_map.93
  23.8 1.1 convert_element_type.24
  25.0 3.9 %all-to-all-start = ((f16[32,17,8,128]{3,2,1,0:T(8,128)(2,1)}), f16[32,17,8,128]{3,2,1,0:T(8,128)(2,1)S(1)}, u32[]{:S(2)}, u32[]{:S(2)}) async-start(f16[32,17,8,128]{3,2,1,0:T(8,128)(2,1)} %bitcast), calls=%async_computation | async-start | bytes 2228224 | tf_op jit(solution)/shard_map/all_to_all | solution.py:27
  28.9 18.2 %all-to-all-done = f16[32,17,8,128]{3,2,1,0:T(8,128)(2,1)S(1)} async-done(((f16[32,17,8,128]{3,2,1,0:T(8,128)(2,1)}), f16[32,17,8,128]{3,2,1,0:T(8,128)(2,1)S(1)}, u32[]{:S(2)}, u32[]{:S(2)}) %all-to-all-start) | async-done | bytes 1114144 | tf_op jit(solution)/shard_map/all_to_all | solution.py:27
  47.6 42.7 %all_to_all.15 = bf16[16,24,128]{2,1,0:T(8,128)(2,1)S(1)} all-to-all(bf16[16,24,128]{2,1,0:T(8,128)(2,1)S(1)} %pad_maximum_fusion.7), channel_id=1, replica_groups=mesh['xh'=2,'c'=2,'y'=4,'zh'=16,'zl'=2,'xl'=2] {'zh'}, dimensions={0} | all-to-all | bytes 196608 | tf_op jit(solution)/shard_map/all_to_all | solution.py:27
  90.3 1.2 broadcast_in_dim.5
  91.5 4.1 %all-to-all-start.2 = ((bf16[32,16,8,128]{3,2,1,0:T(8,128)(2,1)}), bf16[32,16,8,128]{3,2,1,0:T(8,128)(2,1)S(1)}, u32[]{:S(2)}, u32[]{:S(2)}) async-start(bf16[32,16,8,128]{3,2,1,0:T(8,128)(2,1)} %broadcast_in_dim.5), calls=%async_computation.2 | async-start | bytes 2097152 | tf_op jit(solution)/shard_map/all_to_all | solution.py:27
  95.6 4.9 %collective-permute-start.1 = (f32[8,128]{1,0:T(8,128)S(1)}, f32[8,128]{1,0:T(8,128)S(1)}, u32[]{:S(2)}, u32[]{:S(2)}) collective-permute-start(f32[8,128]{1,0:T(8,128)S(1)} %broadcast_multiply_fusion), channel_id=1, source_target_pairs={{0,256},{256,0},{1,257},{257,1},{2,258},{258,2},{3,259},{259,3},{4... | collective-permute-start | bytes 12296 | tf_op jit(solution)/shard_map/ppermute | solution.py:14
  100.5 0.8 collective-permute-done.1
  101.3 4.9 %collective-permute-start.2 = (f32[2,8,128]{2,1,0:T(8,128)S(1)}, f32[2,8,128]{2,1,0:T(8,128)S(1)}, u32[]{:S(2)}, u32[]{:S(2)}) collective-permute-start(f32[2,8,128]{2,1,0:T(8,128)S(1)} %pad_maximum_fusion.9), channel_id=1, source_target_pairs={{0,512},{512,0},{1,513},{513,1},{2,514},{514,2},{3,515},{515,3},{4... | collective-permute-start | bytes 24584 | tf_op jit(solution)/shard_map/ppermute | solution.py:14
  106.2 1.7 %collective-permute-done.2 = f32[2,8,128]{2,1,0:T(8,128)S(1)} collective-permute-done((f32[2,8,128]{2,1,0:T(8,128)S(1)}, f32[2,8,128]{2,1,0:T(8,128)S(1)}, u32[]{:S(2)}, u32[]{:S(2)}) %collective-permute-start.2) | collective-permute-done | bytes 8224 | tf_op jit(solution)/shard_map/ppermute | solution.py:14
  107.9 2.3 %all-to-all-done.2 = bf16[32,16,8,128]{3,2,1,0:T(8,128)(2,1)S(1)} async-done(((bf16[32,16,8,128]{3,2,1,0:T(8,128)(2,1)}), bf16[32,16,8,128]{3,2,1,0:T(8,128)(2,1)S(1)}, u32[]{:S(2)}, u32[]{:S(2)}) %all-to-all-start.2) | async-done | bytes 1048608 | tf_op jit(solution)/shard_map/all_to_all | solution.py:27
  110.2 0.3 copy.12
  110.5 6.1 %collective-permute-start.3 = (bf16[4096,128]{1,0:T(8,128)(2,1)S(1)}, bf16[4096,128]{1,0:T(8,128)(2,1)S(1)}, u32[]{:S(2)}, u32[]{:S(2)}) collective-permute-start(bf16[4096,128]{1,0:T(8,128)(2,1)S(1)} %bitcast.19), channel_id=1, source_target_pairs={{0,256},{256,0},{1,257},{257,1},{2,258},{258,2},{3,259},{259,3},{4... | collective-permute-start | bytes 3145736 | tf_op jit(solution)/shard_map/ppermute | solution.py:14
  116.7 0.6 slice_bitcast_fusion
  117.3 1.7 %collective-permute-done.3 = bf16[4096,128]{1,0:T(8,128)(2,1)S(1)} collective-permute-done((bf16[4096,128]{1,0:T(8,128)(2,1)S(1)}, bf16[4096,128]{1,0:T(8,128)(2,1)S(1)}, u32[]{:S(2)}, u32[]{:S(2)}) %collective-permute-start.3) | collective-permute-done | bytes 1048608 | tf_op jit(solution)/shard_map/ppermute | solution.py:14
  118.9 0.5 fusion.3
  119.4 0.6 broadcast_select_fusion
  120.0 1.8 %convolution_convert_fusion = bf16[128,4096]{1,0:T(8,128)(2,1)} fusion(bf16[4096,128]{1,0:T(8,128)(2,1)S(1)} %collective-permute-done.3, bf16[4096,128]{1,0:T(8,128)(2,1)S(1)} %bitcast.21, bf16[128,128]{1,0:T(8,128)(2,1)S(1)} %get-tuple-element.13.refs_1_, bf16[128,128]{1,0:T(8,128)(2,1)S(1)} %get-tuple-element.14.refs_1_), kind=kOutput, calls=%fused_computation | convolution fusion | flops 273285120 | bytes 3211264 | tf_op jit(solution)/shard_map/dot_general | solution.py:122
  (22 shorter events, 0.5 us)
Async XLA Ops:
  1.4 1.2 %copy-start = (bf16[128,4096]{1,0:T(8,128)(2,1)S(1)}, bf16[128,4096]{1,0:T(8,128)(2,1)}, u32[]{:S(2)}) copy-start(bf16[128,4096]{1,0:T(8,128)(2,1)} %refs_0_.3) | copy-start | bytes 3145732
  3.1 19.8 %collective-permute-start = (f32[2,4,2,2,16,8,128]{6,5,4,3,2,1,0:T(8,128)S(1)}, f32[2,4,2,2,16,8,128]{6,5,4,3,2,1,0:T(8,128)S(1)}, u32[]{:S(2)}, u32[]{:S(2)}) collective-permute-start(f32[2,4,2,2,16,8,128]{6,5,4,3,2,1,0:T(8,128)S(1)} %shard_map.92), channel_id=1, source_target_pairs={{0,256},{256,0},{1,257},{257,1},{2,258},{258,2},{3,259},{259,3},{4... | collective-permute-start | bytes 6291464 | tf_op jit(solution)/shard_map/ppermute | solution.py:14
  23.8 5.1 %copy-start.2 = (bf16[16,128]{1,0:T(8,128)(2,1)S(1)}, bf16[16,128]{1,0:T(8,128)(2,1)}, u32[]{:S(2)}) copy-start(bf16[16,128]{1,0:T(8,128)(2,1)} %param.7) | copy-start | bytes 12292
  23.8 5.1 %copy-start.3 = (bf16[16,128]{1,0:T(8,128)(2,1)S(1)}, bf16[16,128]{1,0:T(8,128)(2,1)}, u32[]{:S(2)}) copy-start(bf16[16,128]{1,0:T(8,128)(2,1)} %param.6) | copy-start | bytes 12292
  25.0 22.2 %all-to-all-start = ((f16[32,17,8,128]{3,2,1,0:T(8,128)(2,1)}), f16[32,17,8,128]{3,2,1,0:T(8,128)(2,1)S(1)}, u32[]{:S(2)}, u32[]{:S(2)}) async-start(f16[32,17,8,128]{3,2,1,0:T(8,128)(2,1)} %bitcast), calls=%async_computation | async-start | bytes 2228224 | tf_op jit(solution)/shard_map/all_to_all | solution.py:27
  91.5 27.4 %copy-start.1 = (bf16[128,4096]{1,0:T(8,128)(2,1)S(1)}, bf16[128,4096]{1,0:T(8,128)(2,1)}, u32[]{:S(2)}) copy-start(bf16[128,4096]{1,0:T(8,128)(2,1)} %refs_0_.3) | copy-start | bytes 3145732
  91.5 18.8 %all-to-all-start.2 = ((bf16[32,16,8,128]{3,2,1,0:T(8,128)(2,1)}), bf16[32,16,8,128]{3,2,1,0:T(8,128)(2,1)S(1)}, u32[]{:S(2)}, u32[]{:S(2)}) async-start(bf16[32,16,8,128]{3,2,1,0:T(8,128)(2,1)} %broadcast_in_dim.5), calls=%async_computation.2 | async-start | bytes 2097152 | tf_op jit(solution)/shard_map/all_to_all | solution.py:27
  95.6 5.7 %collective-permute-start.1 = (f32[8,128]{1,0:T(8,128)S(1)}, f32[8,128]{1,0:T(8,128)S(1)}, u32[]{:S(2)}, u32[]{:S(2)}) collective-permute-start(f32[8,128]{1,0:T(8,128)S(1)} %broadcast_multiply_fusion), channel_id=1, source_target_pairs={{0,256},{256,0},{1,257},{257,1},{2,258},{258,2},{3,259},{259,3},{4... | collective-permute-start | bytes 12296 | tf_op jit(solution)/shard_map/ppermute | solution.py:14
  101.3 6.6 %collective-permute-start.2 = (f32[2,8,128]{2,1,0:T(8,128)S(1)}, f32[2,8,128]{2,1,0:T(8,128)S(1)}, u32[]{:S(2)}, u32[]{:S(2)}) collective-permute-start(f32[2,8,128]{2,1,0:T(8,128)S(1)} %pad_maximum_fusion.9), channel_id=1, source_target_pairs={{0,512},{512,0},{1,513},{513,1},{2,514},{514,2},{3,515},{515,3},{4... | collective-permute-start | bytes 24584 | tf_op jit(solution)/shard_map/ppermute | solution.py:14
  110.5 8.4 %collective-permute-start.3 = (bf16[4096,128]{1,0:T(8,128)(2,1)S(1)}, bf16[4096,128]{1,0:T(8,128)(2,1)S(1)}, u32[]{:S(2)}, u32[]{:S(2)}) collective-permute-start(bf16[4096,128]{1,0:T(8,128)(2,1)S(1)} %bitcast.19), channel_id=1, source_target_pairs={{0,256},{256,0},{1,257},{257,1},{2,258},{258,2},{3,259},{259,3},{4... | collective-permute-start | bytes 3145736 | tf_op jit(solution)/shard_map/ppermute | solution.py:14

commit v6 on v5

--- a/solution.py
+++ b/solution.py
@@ -67,7 +67,7 @@
                         out_ref[i, y, j, low, highs] = level
 
 
-def terms(activations, cotangent, *arrived):
+def terms(activations, cotangent, *others):
     tokens, width = activations.shape
     head = cotangent.shape[1]
     ys, lows, highs = (lax.axis_size(a) for a in ("y", "zl", "zh"))
@@ -75,13 +75,13 @@
     return pl.pallas_call(
         lambda *refs: terms_kernel(highs, *refs),
         out_shape=jax.ShapeDtypeStruct(
-            (2, ys, 2, lows, highs + len(arrived), half, head), jnp.float32
+            (2, ys, 2, lows, highs + len(others), half, head), jnp.float32
         ),
         compiler_params=pltpu.CompilerParams(vmem_limit_bytes=40 * 2**20),
         cost_estimate=pl.CostEstimate(
             flops=2 * tokens * width * head, bytes_accessed=6 * width * head, transcendentals=0
         ),
-    )(activations, cotangent, *arrived)
+    )(activations, cotangent, *others)
 
 
 def body(activations, w_query, w_key, grad_query, grad_key):
@@ -94,8 +94,8 @@
 
     mine = pick(grad_query, grad_key)
     other = pick(grad_key, grad_query)
-    arrived = swap(terms(activations, other), "c")
-    sent = terms(activations, mine, arrived).astype(jnp.float16)
+    activations2, cotangent2 = swap(activations, "c"), swap(other, "c")
+    sent = terms(activations2, cotangent2, terms(activations, mine)).astype(jnp.float16)
     landed = exchange(sent.reshape((near,) + sent.shape[4:]), NEAR).astype(jnp.float32)
     summed = (landed[:, :-1] * jnp.exp2(-landed[:, -1:])).sum(axis=0)
 

time: 122 us -> 118 us (0.967)
  waiting for transfers between devices: 28.4 us -> 23.1 us
  starting transfers between devices: 39.9 us -> 43.5 us
  blocking collectives: 42.7 us -> 40.2 us
    ppermute x4 -> x5, starting transfers between devices: 31.9 us -> 35.5 us  [swap(): return lax.ppermute(block, axis, [(0, 1), (1, 0)])]
    ppermute x4 -> x5, waiting for transfers between devices: 7.92 us -> 4.86 us  [swap(): return lax.ppermute(block, axis, [(0, 1), (1, 0)])]
    all_to_all x1, blocking collectives: 42.7 us -> 40.2 us  [exchange(): return lax.all_to_all(blocks, axes, 0, 0, tiled=True)]
    all_to_all x2, waiting for transfers between devices: 20.5 us -> 18.3 us  [exchange(): return lax.all_to_all(blocks, axes, 0, 0, tiled=True)]
  transfers between devices with their start and end apart: 6 -> 7, of which waited for: 6 -> 4; matrix products, arithmetic and copies ran while one was open for 1% -> 1% of each run, Pallas kernels for 0% -> 0%
where the time goes in v6:
time: 118 us
  starting transfers between devices  43.5 us (37%)
  blocking collectives  40.2 us (34%)
  waiting for transfers between devices  23.1 us (20%)
  local copies, waits for them, and re-layouts  3.35 us (3%)
  other arithmetic  3.06 us (3%)
  matrix products  2.26 us (2%)
  Pallas kernels  1.29 us (1%)
    all_to_all x1, blocking collectives, exchange(): return lax.all_to_all(blocks, axes, 0, 0, tiled=True)  40.2 us
    ppermute x5, starting transfers between devices, swap(): return lax.ppermute(block, axis, [(0, 1), (1, 0)])  35.5 us
    all_to_all x2, waiting for transfers between devices, exchange(): return lax.all_to_all(blocks, axes, 0, 0, tiled=True)  18.3 us
    all_to_all x2, starting transfers between devices, exchange(): return lax.all_to_all(blocks, axes, 0, 0, tiled=True)  8 us
    ppermute x5, waiting for transfers between devices, swap(): return lax.ppermute(block, axis, [(0, 1), (1, 0)])  4.86 us
  transfers between devices with their start and end apart: 7, of which 4 were waited for; matrix products, arithmetic and copies ran while one was open for 1% of the time, Pallas kernels for 0%

profile of v6, /device:TPU:1, one launch (start us, length us, event | category | flops | bytes accessed | tf_op | source)
XLA Modules:
  0.0 117.7 jit_solution(11329055157930822558)
XLA Ops:
  0.6 16.1 %collective-permute-start = (bf16[128,4096]{1,0:T(8,128)(2,1)}, bf16[128,4096]{1,0:T(8,128)(2,1)S(1)}, u32[]{:S(2)}, u32[]{:S(2)}) collective-permute-start(bf16[128,4096]{1,0:T(8,128)(2,1)} %refs_0_.1), channel_id=1, source_target_pairs={{0,256},{256,0},{1,257},{257,1},{2,258},{258,2},{3,259},{259,3},{4... | collective-permute-start | bytes 3145736 | tf_op jit(solution)/shard_map/ppermute | solution.py:14
  16.7 0.8 broadcast_select_fusion.2
  17.5 1.9 %collective-permute-start.1 = (bf16[128,128]{1,0:T(8,128)(2,1)S(1)}, bf16[128,128]{1,0:T(8,128)(2,1)S(1)}, u32[]{:S(2)}, u32[]{:S(2)}) collective-permute-start(bf16[128,128]{1,0:T(8,128)(2,1)S(1)} %get-tuple-element.14), channel_id=1, source_target_pairs={{0,256},{256,0},{1,257},{257,1},{2,258},{258,2},{3,259},{259,3},{4... | collective-permute-start | bytes 98312 | tf_op jit(solution)/shard_map/ppermute | solution.py:14
  19.4 1.2 %copy-done = bf16[128,4096]{1,0:T(8,128)(2,1)S(1)} copy-done((bf16[128,4096]{1,0:T(8,128)(2,1)S(1)}, bf16[128,4096]{1,0:T(8,128)(2,1)}, u32[]{:S(2)}) %copy-start) | copy-done | bytes 1048600
  20.6 0.5 shard_map.92.refs_2_
  21.2 0.8 shard_map.93
  22.0 1.2 convert_element_type.24
  23.2 3.9 %all-to-all-start = ((f16[32,17,8,128]{3,2,1,0:T(8,128)(2,1)}), f16[32,17,8,128]{3,2,1,0:T(8,128)(2,1)S(1)}, u32[]{:S(2)}, u32[]{:S(2)}) async-start(f16[32,17,8,128]{3,2,1,0:T(8,128)(2,1)} %bitcast), calls=%async_computation | async-start | bytes 2228224 | tf_op jit(solution)/shard_map/all_to_all | solution.py:27
  27.1 18.3 %all-to-all-done = f16[32,17,8,128]{3,2,1,0:T(8,128)(2,1)S(1)} async-done(((f16[32,17,8,128]{3,2,1,0:T(8,128)(2,1)}), f16[32,17,8,128]{3,2,1,0:T(8,128)(2,1)S(1)}, u32[]{:S(2)}, u32[]{:S(2)}) %all-to-all-start) | async-done | bytes 1114144 | tf_op jit(solution)/shard_map/all_to_all | solution.py:27
  45.6 0.2 fusion
  45.9 40.2 %all_to_all.15 = bf16[16,24,128]{2,1,0:T(8,128)(2,1)S(1)} all-to-all(bf16[16,24,128]{2,1,0:T(8,128)(2,1)S(1)} %pad_maximum_fusion.7), channel_id=1, replica_groups=mesh['xh'=2,'c'=2,'y'=4,'zh'=16,'zl'=2,'xl'=2] {'zh'}, dimensions={0} | all-to-all | bytes 196608 | tf_op jit(solution)/shard_map/all_to_all | solution.py:27
  86.1 1.2 %broadcast_in_dim.5 = bf16[32,16,8,128]{3,2,1,0:T(8,128)(2,1)} broadcast(bf16[16,8,128]{2,1,0:T(8,128)(2,1)S(1)} %slice.42), dimensions={1,2,3} | broadcast | bytes 1081344 | tf_op jit(solution)/shard_map/broadcast_in_dim | solution.py:31
  87.3 4.1 %all-to-all-start.2 = ((bf16[32,16,8,128]{3,2,1,0:T(8,128)(2,1)}), bf16[32,16,8,128]{3,2,1,0:T(8,128)(2,1)S(1)}, u32[]{:S(2)}, u32[]{:S(2)}) async-start(bf16[32,16,8,128]{3,2,1,0:T(8,128)(2,1)} %broadcast_in_dim.5), calls=%async_computation.2 | async-start | bytes 2097152 | tf_op jit(solution)/shard_map/all_to_all | solution.py:27
  91.4 7.1 %collective-permute-start.2 = (f32[8,128]{1,0:T(8,128)S(1)}, f32[8,128]{1,0:T(8,128)S(1)}, u32[]{:S(2)}, u32[]{:S(2)}) collective-permute-start(f32[8,128]{1,0:T(8,128)S(1)} %broadcast_multiply_fusion), channel_id=1, source_target_pairs={{0,256},{256,0},{1,257},{257,1},{2,258},{258,2},{3,259},{259,3},{4... | collective-permute-start | bytes 12296 | tf_op jit(solution)/shard_map/ppermute | solution.py:14
  98.5 0.8 collective-permute-done.2
  99.3 4.9 %collective-permute-start.3 = (f32[2,8,128]{2,1,0:T(8,128)S(1)}, f32[2,8,128]{2,1,0:T(8,128)S(1)}, u32[]{:S(2)}, u32[]{:S(2)}) collective-permute-start(f32[2,8,128]{2,1,0:T(8,128)S(1)} %pad_maximum_fusion.9), channel_id=1, source_target_pairs={{0,512},{512,0},{1,513},{513,1},{2,514},{514,2},{3,515},{515,3},{4... | collective-permute-start | bytes 24584 | tf_op jit(solution)/shard_map/ppermute | solution.py:14
  104.2 2.4 %collective-permute-done.3 = f32[2,8,128]{2,1,0:T(8,128)S(1)} collective-permute-done((f32[2,8,128]{2,1,0:T(8,128)S(1)}, f32[2,8,128]{2,1,0:T(8,128)S(1)}, u32[]{:S(2)}, u32[]{:S(2)}) %collective-permute-start.3) | collective-permute-done | bytes 8224 | tf_op jit(solution)/shard_map/ppermute | solution.py:14
  106.6 0.3 copy.12
  106.9 5.6 %collective-permute-start.4 = (bf16[4096,128]{1,0:T(8,128)(2,1)S(1)}, bf16[4096,128]{1,0:T(8,128)(2,1)S(1)}, u32[]{:S(2)}, u32[]{:S(2)}) collective-permute-start(bf16[4096,128]{1,0:T(8,128)(2,1)S(1)} %bitcast.19), channel_id=1, source_target_pairs={{0,256},{256,0},{1,257},{257,1},{2,258},{258,2},{3,259},{259,3},{4... | collective-permute-start | bytes 3145736 | tf_op jit(solution)/shard_map/ppermute | solution.py:14
  112.5 0.6 slice_bitcast_fusion
  113.1 1.7 %collective-permute-done.4 = bf16[4096,128]{1,0:T(8,128)(2,1)S(1)} collective-permute-done((bf16[4096,128]{1,0:T(8,128)(2,1)S(1)}, bf16[4096,128]{1,0:T(8,128)(2,1)S(1)}, u32[]{:S(2)}, u32[]{:S(2)}) %collective-permute-start.4) | collective-permute-done | bytes 1048608 | tf_op jit(solution)/shard_map/ppermute | solution.py:14
  114.8 0.5 fusion.3
  115.2 0.6 broadcast_select_fusion
  115.9 1.8 %convolution_convert_fusion = bf16[128,4096]{1,0:T(8,128)(2,1)} fusion(bf16[4096,128]{1,0:T(8,128)(2,1)S(1)} %collective-permute-done.4, bf16[4096,128]{1,0:T(8,128)(2,1)S(1)} %bitcast.21, bf16[128,128]{1,0:T(8,128)(2,1)S(1)} %get-tuple-element.14, bf16[128,128]{1,0:T(8,128)(2,1)S(1)} %get-tuple-element.13.refs_1_), kind=kOutput, calls=%fused_computation | convolution fusion | flops 273285120 | bytes 3211264 | tf_op jit(solution)/shard_map/dot_general | solution.py:122
  (24 shorter events, 0.3 us)
Async XLA Ops:
  0.6 20.5 %collective-permute-start = (bf16[128,4096]{1,0:T(8,128)(2,1)}, bf16[128,4096]{1,0:T(8,128)(2,1)S(1)}, u32[]{:S(2)}, u32[]{:S(2)}) collective-permute-start(bf16[128,4096]{1,0:T(8,128)(2,1)} %refs_0_.1), channel_id=1, source_target_pairs={{0,256},{256,0},{1,257},{257,1},{2,258},{258,2},{3,259},{259,3},{4... | collective-permute-start | bytes 3145736 | tf_op jit(solution)/shard_map/ppermute | solution.py:14
  17.5 3.6 %collective-permute-start.1 = (bf16[128,128]{1,0:T(8,128)(2,1)S(1)}, bf16[128,128]{1,0:T(8,128)(2,1)S(1)}, u32[]{:S(2)}, u32[]{:S(2)}) collective-permute-start(bf16[128,128]{1,0:T(8,128)(2,1)S(1)} %get-tuple-element.14), channel_id=1, source_target_pairs={{0,256},{256,0},{1,257},{257,1},{2,258},{258,2},{3,259},{259,3},{4... | collective-permute-start | bytes 98312 | tf_op jit(solution)/shard_map/ppermute | solution.py:14
  19.4 1.2 %copy-start = (bf16[128,4096]{1,0:T(8,128)(2,1)S(1)}, bf16[128,4096]{1,0:T(8,128)(2,1)}, u32[]{:S(2)}) copy-start(bf16[128,4096]{1,0:T(8,128)(2,1)} %refs_0_.1) | copy-start | bytes 3145732
  22.0 5.1 %copy-start.2 = (bf16[16,128]{1,0:T(8,128)(2,1)S(1)}, bf16[16,128]{1,0:T(8,128)(2,1)}, u32[]{:S(2)}) copy-start(bf16[16,128]{1,0:T(8,128)(2,1)} %param.7) | copy-start | bytes 12292
  22.0 5.1 %copy-start.3 = (bf16[16,128]{1,0:T(8,128)(2,1)S(1)}, bf16[16,128]{1,0:T(8,128)(2,1)}, u32[]{:S(2)}) copy-start(bf16[16,128]{1,0:T(8,128)(2,1)} %param.6) | copy-start | bytes 12292
  23.2 22.2 %all-to-all-start = ((f16[32,17,8,128]{3,2,1,0:T(8,128)(2,1)}), f16[32,17,8,128]{3,2,1,0:T(8,128)(2,1)S(1)}, u32[]{:S(2)}, u32[]{:S(2)}) async-start(f16[32,17,8,128]{3,2,1,0:T(8,128)(2,1)} %bitcast), calls=%async_computation | async-start | bytes 2228224 | tf_op jit(solution)/shard_map/all_to_all | solution.py:27
  87.3 27.5 %copy-start.1 = (bf16[128,4096]{1,0:T(8,128)(2,1)S(1)}, bf16[128,4096]{1,0:T(8,128)(2,1)}, u32[]{:S(2)}) copy-start(bf16[128,4096]{1,0:T(8,128)(2,1)} %refs_0_.1) | copy-start | bytes 3145732
  87.3 19.4 %all-to-all-start.2 = ((bf16[32,16,8,128]{3,2,1,0:T(8,128)(2,1)}), bf16[32,16,8,128]{3,2,1,0:T(8,128)(2,1)S(1)}, u32[]{:S(2)}, u32[]{:S(2)}) async-start(bf16[32,16,8,128]{3,2,1,0:T(8,128)(2,1)} %broadcast_in_dim.5), calls=%async_computation.2 | async-start | bytes 2097152 | tf_op jit(solution)/shard_map/all_to_all | solution.py:27
  91.4 7.9 %collective-permute-start.2 = (f32[8,128]{1,0:T(8,128)S(1)}, f32[8,128]{1,0:T(8,128)S(1)}, u32[]{:S(2)}, u32[]{:S(2)}) collective-permute-start(f32[8,128]{1,0:T(8,128)S(1)} %broadcast_multiply_fusion), channel_id=1, source_target_pairs={{0,256},{256,0},{1,257},{257,1},{2,258},{258,2},{3,259},{259,3},{4... | collective-permute-start | bytes 12296 | tf_op jit(solution)/shard_map/ppermute | solution.py:14
  99.3 7.3 %collective-permute-start.3 = (f32[2,8,128]{2,1,0:T(8,128)S(1)}, f32[2,8,128]{2,1,0:T(8,128)S(1)}, u32[]{:S(2)}, u32[]{:S(2)}) collective-permute-start(f32[2,8,128]{2,1,0:T(8,128)S(1)} %pad_maximum_fusion.9), channel_id=1, source_target_pairs={{0,512},{512,0},{1,513},{513,1},{2,514},{514,2},{3,515},{515,3},{4... | collective-permute-start | bytes 24584 | tf_op jit(solution)/shard_map/ppermute | solution.py:14
  106.9 7.8 %collective-permute-start.4 = (bf16[4096,128]{1,0:T(8,128)(2,1)S(1)}, bf16[4096,128]{1,0:T(8,128)(2,1)S(1)}, u32[]{:S(2)}, u32[]{:S(2)}) collective-permute-start(bf16[4096,128]{1,0:T(8,128)(2,1)S(1)} %bitcast.19), channel_id=1, source_target_pairs={{0,256},{256,0},{1,257},{257,1},{2,258},{258,2},{3,259},{259,3},{4... | collective-permute-start | bytes 3145736 | tf_op jit(solution)/shard_map/ppermute | solution.py:14

commit v7 on v6

--- a/solution.py
+++ b/solution.py
@@ -31,19 +31,19 @@
     return jnp.broadcast_to(block[None], (count,) + block.shape)
 
 
-def terms_kernel(highs, act_ref, cot_ref, *refs):
+def terms_kernel(highs, width, act_ref, cot_ref, *refs):
     out_ref = refs[-1]
     _, ys, _, lows, _, half, head = out_ref.shape
     cut = 2
     span = highs // cut
-    block = act_ref.shape[1] // (ys * cut)
+    block = width // (ys * cut)
     peak = jnp.zeros((half, head), jnp.float32)
     for y in range(ys):
         for z in range(cut):
             start = (y * cut + z) * block
             part = lax.dot_general(
                 act_ref[:, start : start + block],
-                cot_ref[...],
+                cot_ref[:, cot_ref.shape[1] - head :],
                 (((0,), (0,)), ((), ())),
                 preferred_element_type=jnp.float32,
             ).reshape(span, lows, 2, 2, half, head)
@@ -67,13 +67,12 @@
                         out_ref[i, y, j, low, highs] = level
 
 
-def terms(activations, cotangent, *others):
-    tokens, width = activations.shape
-    head = cotangent.shape[1]
+def terms(joined, cotangent, width, head, *others):
+    tokens = joined.shape[0]
     ys, lows, highs = (lax.axis_size(a) for a in ("y", "zl", "zh"))
     half = width // (4 * ys * lows * highs)
     return pl.pallas_call(
-        lambda *refs: terms_kernel(highs, *refs),
+        lambda *refs: terms_kernel(highs, width, *refs),
         out_shape=jax.ShapeDtypeStruct(
             (2, ys, 2, lows, highs + len(others), half, head), jnp.float32
         ),
@@ -81,7 +80,64 @@
         cost_estimate=pl.CostEstimate(
             flops=2 * tokens * width * head, bytes_accessed=6 * width * head, transcendentals=0
         ),
-    )(activations, cotangent, *others)
+    )(joined, cotangent, *others)
+
+
+def finish_kernel(core_ref, act_ref, own_ref, came_ref, mine_ref, other_ref, *refs):
+    query_ref, key_ref, grad_ref, held_ref, sems = refs
+    count = sems.shape[0]
+    block = own_ref.shape[0] // count
+    sends = []
+    for i in range(count):
+        span = pl.ds(i * block, block)
+        grad = sum(
+            lax.dot_general(
+                cot[...], weights[span], (((1,), (1,)), ((), ())), preferred_element_type=jnp.float32
+            )
+            for cot, weights in ((mine_ref, own_ref), (other_ref, came_ref))
+        )
+        held_ref[:, span] = grad.astype(held_ref.dtype)
+        send = pltpu.make_async_copy(held_ref.at[:, span], grad_ref.at[:, span], sems.at[i])
+        send.start()
+        sends.append(send)
+    own, came = (
+        jnp.dot(act_ref[...], weights[...], preferred_element_type=jnp.float32).astype(query_ref.dtype)
+        for weights in (own_ref, came_ref)
+    )
+
+    @pl.when(core_ref[0] == 0)
+    def _():
+        query_ref[...] = own
+        key_ref[...] = came
+
+    @pl.when(core_ref[0] != 0)
+    def _():
+        query_ref[...] = came
+        key_ref[...] = own
+
+    for send in sends:
+        send.wait()
+
+
+def finish(activations, sheet, other_sheet, mine, other):
+    tokens, width = activations.shape
+    head = sheet.shape[1]
+    dtype = activations.dtype
+    count = 8
+    core = lax.axis_index("c").astype(jnp.int32).reshape(1)
+    out = jax.ShapeDtypeStruct((tokens, head), dtype)
+    return pl.pallas_call(
+        finish_kernel,
+        in_specs=[pl.BlockSpec(memory_space=pltpu.SMEM)]
+        + [pl.BlockSpec(memory_space=pltpu.VMEM)] * 5,
+        out_specs=[pl.BlockSpec(memory_space=pltpu.VMEM)] * 2 + [pl.BlockSpec(memory_space=pl.ANY)],
+        out_shape=(out, out, jax.ShapeDtypeStruct((tokens, width), dtype)),
+        scratch_shapes=[pltpu.VMEM((tokens, width), dtype), pltpu.SemaphoreType.DMA((count,))],
+        compiler_params=pltpu.CompilerParams(vmem_limit_bytes=40 * 2**20),
+        cost_estimate=pl.CostEstimate(
+            flops=8 * tokens * width * head, bytes_accessed=8 * tokens * width, transcendentals=0
+        ),
+    )(core, activations, sheet, other_sheet, mine, other)
 
 
 def body(activations, w_query, w_key, grad_query, grad_key):
@@ -94,8 +150,9 @@
 
     mine = pick(grad_query, grad_key)
     other = pick(grad_key, grad_query)
-    activations2, cotangent2 = swap(activations, "c"), swap(other, "c")
-    sent = terms(activations2, cotangent2, terms(activations, mine)).astype(jnp.float16)
+    joined = jnp.concatenate([activations, other], axis=1)
+    came = swap(joined, "c")
+    sent = terms(came, came, width, head, terms(joined, mine, width, head)).astype(jnp.float16)
     landed = exchange(sent.reshape((near,) + sent.shape[4:]), NEAR).astype(jnp.float32)
     summed = (landed[:, :-1] * jnp.exp2(-landed[:, -1:])).sum(axis=0)
 
@@ -116,14 +173,8 @@
     sheet = sheet.reshape(width, head)
     other_sheet = swap(sheet, "c")
 
-    weights = jnp.concatenate([sheet, other_sheet], axis=1)
-    cotangent = jnp.concatenate([mine, other], axis=1)
-    projected = jnp.dot(activations, weights, preferred_element_type=jnp.float32).astype(jnp.bfloat16)
-    grad_input = lax.dot_general(
-        cotangent, weights, (((1,), (1,)), ((), ())), preferred_element_type=jnp.float32
-    ).astype(jnp.bfloat16)
-    first, second = projected[:, :head], projected[:, head:]
-    return (pick(first, second), pick(second, first), grad_input, whole[0], whole[1])
+    query_out, key_out, grad_input = finish(activations, sheet, other_sheet, mine, other)
+    return (query_out, key_out, grad_input, whole[0], whole[1])
 
 
 def solution(mesh):

time: 118 us -> 120 us (1.017)
  starting transfers between devices: 43.5 us -> 39.9 us
  waiting for transfers between devices: 23.1 us -> 26.5 us
  blocking collectives: 40.2 us -> 42.7 us
  Pallas kernels: 1.29 us -> 3.75 us
  matrix products: 2.26 us -> 0 us
  local copies, waits for them, and re-layouts: 3.35 us -> 2.13 us
    ppermute x5 -> x4, starting transfers between devices: 35.5 us -> 31.9 us  [swap(): return lax.ppermute(block, axis, [(0, 1), (1, 0)])]
    all_to_all x1, blocking collectives: 40.2 us -> 42.7 us  [exchange(): return lax.all_to_all(blocks, axes, 0, 0, tiled=True)]
    pallas_call x2 -> x3, Pallas kernels: 1.29 us -> 3.75 us  [the longest x1 2.48 us: finish(): pl.pallas_call(finish_kernel, in_specs=[pl.BlockSpec(memory_space=pltpu.S...]
    dot_general x2 -> x0, matrix products: 2.26 us -> none  [the longest x1 1.79 us: body(): lax.dot_general(cotangent, weights, (((1,), (1,)), ((), ())), preferred_e...]
    all_to_all x2, waiting for transfers between devices: 18.3 us -> 20.5 us  [exchange(): return lax.all_to_all(blocks, axes, 0, 0, tiled=True)]
    concatenate x0 -> x1, other arithmetic: none -> 1.3 us  [body(): joined = jnp.concatenate([activations, other], axis=1)]
    unnamed x8 -> x6, local copies, waits for them, and re-layouts: 1.24 us -> 0.02 us
    ppermute x5 -> x4, waiting for transfers between devices: 4.86 us -> 5.98 us  [swap(): return lax.ppermute(block, axis, [(0, 1), (1, 0)])]
  transfers between devices with their start and end apart: 7 -> 6, of which waited for: 4 -> 6; matrix products, arithmetic and copies ran while one was open for 1% -> 1% of each run, Pallas kernels for 0% -> 0%
where the time goes in v7:
time: 120 us
  blocking collectives  42.7 us (36%)
  starting transfers between devices  39.9 us (33%)
  waiting for transfers between devices  26.5 us (22%)
  Pallas kernels  3.75 us (3%)
  other arithmetic  3.72 us (3%)
  local copies, waits for them, and re-layouts  2.13 us (2%)
    all_to_all x1, blocking collectives, exchange(): return lax.all_to_all(blocks, axes, 0, 0, tiled=True)  42.7 us
    ppermute x4, starting transfers between devices, swap(): return lax.ppermute(block, axis, [(0, 1), (1, 0)])  31.9 us
    all_to_all x2, waiting for transfers between devices, exchange(): return lax.all_to_all(blocks, axes, 0, 0, tiled=True)  20.5 us
    all_to_all x2, starting transfers between devices, exchange(): return lax.all_to_all(blocks, axes, 0, 0, tiled=True)  8 us
    ppermute x4, waiting for transfers between devices, swap(): return lax.ppermute(block, axis, [(0, 1), (1, 0)])  5.98 us
    pallas_call x1, Pallas kernels, finish(): pl.pallas_call(finish_kernel, in_specs=[pl.BlockSpec(memory_space=pltpu.S...  2.48 us
  transfers between devices with their start and end apart: 6, of which 6 were waited for; matrix products, arithmetic and copies ran while one was open for 1% of the time, Pallas kernels for 0%

profile of v7, /device:TPU:1, one launch (start us, length us, event | category | flops | bytes accessed | tf_op | source)
XLA Modules:
  0.0 119.5 jit_solution(779250681978298589)
XLA Ops:
  0.6 0.8 broadcast_select_fusion
  1.4 1.3 %pad_maximum_fusion.refs_0_ = bf16[128,4224]{1,0:T(8,128)(2,1)S(1)} fusion(bf16[128,128]{1,0:T(8,128)(2,1)S(1)} %get-tuple-element.18.other_ref, bf16[128,4096]{1,0:T(8,128)(2,1)} %act_ref.1), kind=kLoop, calls=%fused_computation.2 | loop fusion | flops 2162688 | bytes 2162688 | tf_op jit(solution)/shard_map/concatenate | solution.py:153
  2.7 16.1 %collective-permute-start = (bf16[128,4224]{1,0:T(8,128)(2,1)S(1)}, bf16[128,4224]{1,0:T(8,128)(2,1)S(1)}, u32[]{:S(2)}, u32[]{:S(2)}) collective-permute-start(bf16[128,4224]{1,0:T(8,128)(2,1)S(1)} %pad_maximum_fusion.refs_0_), channel_id=1, source_target_pairs={{0,256},{256,0},{1,257},{257,1},{2,258},{258,2},{3,259},{259,3},{4... | collective-permute-start | bytes 3244040 | tf_op jit(solution)/shard_map/ppermute | solution.py:14
  18.8 0.5 shard_map.92.refs_2_
  19.3 1.8 %collective-permute-done.refs_0_.refs_1_ = bf16[128,4224]{1,0:T(8,128)(2,1)S(1)} collective-permute-done((bf16[128,4224]{1,0:T(8,128)(2,1)S(1)}, bf16[128,4224]{1,0:T(8,128)(2,1)S(1)}, u32[]{:S(2)}, u32[]{:S(2)}) %collective-permute-start) | collective-permute-done | bytes 1081376 | tf_op jit(solution)/shard_map/ppermute | solution.py:14
  21.1 0.8 shard_map.93
  21.9 1.1 convert_element_type.15
  23.1 3.9 %all-to-all-start = ((f16[32,17,8,128]{3,2,1,0:T(8,128)(2,1)}), f16[32,17,8,128]{3,2,1,0:T(8,128)(2,1)S(1)}, u32[]{:S(2)}, u32[]{:S(2)}) async-start(f16[32,17,8,128]{3,2,1,0:T(8,128)(2,1)} %bitcast.1), calls=%async_computation | async-start | bytes 2228224 | tf_op jit(solution)/shard_map/all_to_all | solution.py:27
  27.1 18.2 %all-to-all-done = f16[32,17,8,128]{3,2,1,0:T(8,128)(2,1)S(1)} async-done(((f16[32,17,8,128]{3,2,1,0:T(8,128)(2,1)}), f16[32,17,8,128]{3,2,1,0:T(8,128)(2,1)S(1)}, u32[]{:S(2)}, u32[]{:S(2)}) %all-to-all-start) | async-done | bytes 1114144 | tf_op jit(solution)/shard_map/all_to_all | solution.py:27
  45.3 0.1 convert_element_type.16
  45.4 0.2 fusion
  45.7 42.7 %all_to_all.15 = bf16[16,24,128]{2,1,0:T(8,128)(2,1)S(1)} all-to-all(bf16[16,24,128]{2,1,0:T(8,128)(2,1)S(1)} %pad_maximum_fusion.1), channel_id=1, replica_groups=mesh['xh'=2,'c'=2,'y'=4,'zh'=16,'zl'=2,'xl'=2] {'zh'}, dimensions={0} | all-to-all | bytes 196608 | tf_op jit(solution)/shard_map/all_to_all | solution.py:27
  88.4 1.2 %broadcast_in_dim.5 = bf16[32,16,8,128]{3,2,1,0:T(8,128)(2,1)} broadcast(bf16[16,8,128]{2,1,0:T(8,128)(2,1)S(1)} %slice.34), dimensions={1,2,3} | broadcast | bytes 1081344 | tf_op jit(solution)/shard_map/broadcast_in_dim | solution.py:31
  89.6 4.1 %all-to-all-start.2 = ((bf16[32,16,8,128]{3,2,1,0:T(8,128)(2,1)}), bf16[32,16,8,128]{3,2,1,0:T(8,128)(2,1)S(1)}, u32[]{:S(2)}, u32[]{:S(2)}) async-start(bf16[32,16,8,128]{3,2,1,0:T(8,128)(2,1)} %broadcast_in_dim.5), calls=%async_computation.2 | async-start | bytes 2097152 | tf_op jit(solution)/shard_map/all_to_all | solution.py:27
  93.7 4.9 %collective-permute-start.1 = (f32[8,128]{1,0:T(8,128)S(1)}, f32[8,128]{1,0:T(8,128)S(1)}, u32[]{:S(2)}, u32[]{:S(2)}) collective-permute-start(f32[8,128]{1,0:T(8,128)S(1)} %broadcast_multiply_fusion), channel_id=1, source_target_pairs={{0,256},{256,0},{1,257},{257,1},{2,258},{258,2},{3,259},{259,3},{4... | collective-permute-start | bytes 12296 | tf_op jit(solution)/shard_map/ppermute | solution.py:14
  98.6 0.8 collective-permute-done.1
  99.4 4.9 %collective-permute-start.2 = (f32[2,8,128]{2,1,0:T(8,128)S(1)}, f32[2,8,128]{2,1,0:T(8,128)S(1)}, u32[]{:S(2)}, u32[]{:S(2)}) collective-permute-start(f32[2,8,128]{2,1,0:T(8,128)S(1)} %pad_maximum_fusion.3), channel_id=1, source_target_pairs={{0,512},{512,0},{1,513},{513,1},{2,514},{514,2},{3,515},{515,3},{4... | collective-permute-start | bytes 24584 | tf_op jit(solution)/shard_map/ppermute | solution.py:14
  104.3 1.7 %collective-permute-done.2 = f32[2,8,128]{2,1,0:T(8,128)S(1)} collective-permute-done((f32[2,8,128]{2,1,0:T(8,128)S(1)}, f32[2,8,128]{2,1,0:T(8,128)S(1)}, u32[]{:S(2)}, u32[]{:S(2)}) %collective-permute-start.2) | collective-permute-done | bytes 8224 | tf_op jit(solution)/shard_map/ppermute | solution.py:14
  106.1 2.3 %all-to-all-done.2 = bf16[32,16,8,128]{3,2,1,0:T(8,128)(2,1)S(1)} async-done(((bf16[32,16,8,128]{3,2,1,0:T(8,128)(2,1)}), bf16[32,16,8,128]{3,2,1,0:T(8,128)(2,1)S(1)}, u32[]{:S(2)}, u32[]{:S(2)}) %all-to-all-start.2) | async-done | bytes 1048608 | tf_op jit(solution)/shard_map/all_to_all | solution.py:27
  108.4 0.3 copy.10
  108.7 6.1 %collective-permute-start.3 = (bf16[4096,128]{1,0:T(8,128)(2,1)S(1)}, bf16[4096,128]{1,0:T(8,128)(2,1)S(1)}, u32[]{:S(2)}, u32[]{:S(2)}) collective-permute-start(bf16[4096,128]{1,0:T(8,128)(2,1)S(1)} %bitcast.16), channel_id=1, source_target_pairs={{0,256},{256,0},{1,257},{257,1},{2,258},{258,2},{3,259},{259,3},{4... | collective-permute-start | bytes 3145736 | tf_op jit(solution)/shard_map/ppermute | solution.py:14
  114.8 0.6 slice_bitcast_fusion
  115.4 1.7 %collective-permute-done.3.came_ref = bf16[4096,128]{1,0:T(8,128)(2,1)S(1)} collective-permute-done((bf16[4096,128]{1,0:T(8,128)(2,1)S(1)}, bf16[4096,128]{1,0:T(8,128)(2,1)S(1)}, u32[]{:S(2)}, u32[]{:S(2)}) %collective-permute-start.3) | collective-permute-done | bytes 1048608 | tf_op jit(solution)/shard_map/ppermute | solution.py:14
  117.1 2.5 %shard_map.94 = (bf16[128,128]{1,0:T(8,128)(2,1)}, bf16[128,128]{1,0:T(8,128)(2,1)}, bf16[128,4096]{1,0:T(8,128)(2,1)}) custom-call(s32[1]{0:T(128)} %bitcast.core_ref, bf16[128,4096]{1,0:T(8,128)(2,1)S(1)} %copy-done, bf16[4096,128]{1,0:T(8,128)(2,1)S(1)} %bitcast.17, bf16[4096,128]{1,0:T(8,128)(2,1)S(1)} %collective-permute-done.3.came_ref, ...), custom_call_target="tpu_custom_call" | custom-call | flops 536870912 | bytes 4194304 | tf_op jit(solution)/shard_map/pallas_call | solution.py:129
  (19 shorter events, 0.2 us)
Async XLA Ops:
  2.7 18.4 %collective-permute-start = (bf16[128,4224]{1,0:T(8,128)(2,1)S(1)}, bf16[128,4224]{1,0:T(8,128)(2,1)S(1)}, u32[]{:S(2)}, u32[]{:S(2)}) collective-permute-start(bf16[128,4224]{1,0:T(8,128)(2,1)S(1)} %pad_maximum_fusion.refs_0_), channel_id=1, source_target_pairs={{0,256},{256,0},{1,257},{257,1},{2,258},{258,2},{3,259},{259,3},{4... | collective-permute-start | bytes 3244040 | tf_op jit(solution)/shard_map/ppermute | solution.py:14
  21.9 5.1 %copy-start.1 = (bf16[16,128]{1,0:T(8,128)(2,1)S(1)}, bf16[16,128]{1,0:T(8,128)(2,1)}, u32[]{:S(2)}) copy-start(bf16[16,128]{1,0:T(8,128)(2,1)} %param.7) | copy-start | bytes 12292
  21.9 5.1 %copy-start.2 = (bf16[16,128]{1,0:T(8,128)(2,1)S(1)}, bf16[16,128]{1,0:T(8,128)(2,1)}, u32[]{:S(2)}) copy-start(bf16[16,128]{1,0:T(8,128)(2,1)} %param.6) | copy-start | bytes 12292
  23.1 22.2 %all-to-all-start = ((f16[32,17,8,128]{3,2,1,0:T(8,128)(2,1)}), f16[32,17,8,128]{3,2,1,0:T(8,128)(2,1)S(1)}, u32[]{:S(2)}, u32[]{:S(2)}) async-start(f16[32,17,8,128]{3,2,1,0:T(8,128)(2,1)} %bitcast.1), calls=%async_computation | async-start | bytes 2228224 | tf_op jit(solution)/shard_map/all_to_all | solution.py:27
  89.6 27.4 %copy-start = (bf16[128,4096]{1,0:T(8,128)(2,1)S(1)}, bf16[128,4096]{1,0:T(8,128)(2,1)}, u32[]{:S(2)}) copy-start(bf16[128,4096]{1,0:T(8,128)(2,1)} %act_ref.1) | copy-start | bytes 3145732
  89.6 18.8 %all-to-all-start.2 = ((bf16[32,16,8,128]{3,2,1,0:T(8,128)(2,1)}), bf16[32,16,8,128]{3,2,1,0:T(8,128)(2,1)S(1)}, u32[]{:S(2)}, u32[]{:S(2)}) async-start(bf16[32,16,8,128]{3,2,1,0:T(8,128)(2,1)} %broadcast_in_dim.5), calls=%async_computation.2 | async-start | bytes 2097152 | tf_op jit(solution)/shard_map/all_to_all | solution.py:27
  93.7 5.7 %collective-permute-start.1 = (f32[8,128]{1,0:T(8,128)S(1)}, f32[8,128]{1,0:T(8,128)S(1)}, u32[]{:S(2)}, u32[]{:S(2)}) collective-permute-start(f32[8,128]{1,0:T(8,128)S(1)} %broadcast_multiply_fusion), channel_id=1, source_target_pairs={{0,256},{256,0},{1,257},{257,1},{2,258},{258,2},{3,259},{259,3},{4... | collective-permute-start | bytes 12296 | tf_op jit(solution)/shard_map/ppermute | solution.py:14
  99.4 6.6 %collective-permute-start.2 = (f32[2,8,128]{2,1,0:T(8,128)S(1)}, f32[2,8,128]{2,1,0:T(8,128)S(1)}, u32[]{:S(2)}, u32[]{:S(2)}) collective-permute-start(f32[2,8,128]{2,1,0:T(8,128)S(1)} %pad_maximum_fusion.3), channel_id=1, source_target_pairs={{0,512},{512,0},{1,513},{513,1},{2,514},{514,2},{3,515},{515,3},{4... | collective-permute-start | bytes 24584 | tf_op jit(solution)/shard_map/ppermute | solution.py:14
  108.7 8.4 %collective-permute-start.3 = (bf16[4096,128]{1,0:T(8,128)(2,1)S(1)}, bf16[4096,128]{1,0:T(8,128)(2,1)S(1)}, u32[]{:S(2)}, u32[]{:S(2)}) collective-permute-start(bf16[4096,128]{1,0:T(8,128)(2,1)S(1)} %bitcast.16), channel_id=1, source_target_pairs={{0,256},{256,0},{1,257},{257,1},{2,258},{258,2},{3,259},{259,3},{4... | collective-permute-start | bytes 3145736 | tf_op jit(solution)/shard_map/ppermute | solution.py:14

commit v8 on v7

--- a/solution.py
+++ b/solution.py
@@ -31,19 +31,24 @@
     return jnp.broadcast_to(block[None], (count,) + block.shape)
 
 
-def terms_kernel(highs, width, act_ref, cot_ref, *refs):
+def columns(core, width, head):
+    return pl.ds(pl.multiple_of(width + core * head, head), head)
+
+
+def terms_kernel(highs, width, core_ref, act_ref, *refs):
     out_ref = refs[-1]
     _, ys, _, lows, _, half, head = out_ref.shape
     cut = 2
     span = highs // cut
     block = width // (ys * cut)
+    cotangent = act_ref[:, columns(core_ref[0], width, head)]
     peak = jnp.zeros((half, head), jnp.float32)
     for y in range(ys):
         for z in range(cut):
             start = (y * cut + z) * block
             part = lax.dot_general(
                 act_ref[:, start : start + block],
-                cot_ref[:, cot_ref.shape[1] - head :],
+                cotangent,
                 (((0,), (0,)), ((), ())),
                 preferred_element_type=jnp.float32,
             ).reshape(span, lows, 2, 2, half, head)
@@ -67,12 +72,14 @@
                         out_ref[i, y, j, low, highs] = level
 
 
-def terms(joined, cotangent, width, head, *others):
+def terms(core, joined, width, head, *others):
     tokens = joined.shape[0]
     ys, lows, highs = (lax.axis_size(a) for a in ("y", "zl", "zh"))
     half = width // (4 * ys * lows * highs)
     return pl.pallas_call(
         lambda *refs: terms_kernel(highs, width, *refs),
+        in_specs=[pl.BlockSpec(memory_space=pltpu.SMEM)]
+        + [pl.BlockSpec(memory_space=pltpu.VMEM)] * (1 + len(others)),
         out_shape=jax.ShapeDtypeStruct(
             (2, ys, 2, lows, highs + len(others), half, head), jnp.float32
         ),
@@ -80,30 +87,33 @@
         cost_estimate=pl.CostEstimate(
             flops=2 * tokens * width * head, bytes_accessed=6 * width * head, transcendentals=0
         ),
-    )(joined, cotangent, *others)
-
-
-def finish_kernel(core_ref, act_ref, own_ref, came_ref, mine_ref, other_ref, *refs):
+    )(core, joined, *others)
+
+
+def finish_kernel(core_ref, joined_ref, own_ref, came_ref, *refs):
     query_ref, key_ref, grad_ref, held_ref, sems = refs
     count = sems.shape[0]
-    block = own_ref.shape[0] // count
+    width, head = own_ref.shape
+    block = width // count
+    core = core_ref[0]
+    cotangent = jnp.concatenate(
+        [joined_ref[:, columns(index, width, head)] for index in (core, 1 - core)], axis=1
+    )
+    projected = jnp.zeros((joined_ref.shape[0], 2 * head), jnp.float32)
     sends = []
     for i in range(count):
         span = pl.ds(i * block, block)
-        grad = sum(
-            lax.dot_general(
-                cot[...], weights[span], (((1,), (1,)), ((), ())), preferred_element_type=jnp.float32
-            )
-            for cot, weights in ((mine_ref, own_ref), (other_ref, came_ref))
+        weights = jnp.concatenate([own_ref[span], came_ref[span]], axis=1)
+        grad = lax.dot_general(
+            cotangent, weights, (((1,), (1,)), ((), ())), preferred_element_type=jnp.float32
         )
         held_ref[:, span] = grad.astype(held_ref.dtype)
         send = pltpu.make_async_copy(held_ref.at[:, span], grad_ref.at[:, span], sems.at[i])
         send.start()
         sends.append(send)
-    own, came = (
-        jnp.dot(act_ref[...], weights[...], preferred_element_type=jnp.float32).astype(query_ref.dtype)
-        for weights in (own_ref, came_ref)
-    )
+        projected += jnp.dot(joined_ref[:, span], weights, preferred_element_type=jnp.float32)
+    projected = projected.astype(query_ref.dtype)
+    own, came = projected[:, :head], projected[:, head:]
 
     @pl.when(core_ref[0] == 0)
     def _():
@@ -119,17 +129,16 @@
         send.wait()
 
 
-def finish(activations, sheet, other_sheet, mine, other):
-    tokens, width = activations.shape
-    head = sheet.shape[1]
-    dtype = activations.dtype
+def finish(core, joined, sheet, other_sheet):
+    tokens = joined.shape[0]
+    width, head = sheet.shape
+    dtype = joined.dtype
     count = 8
-    core = lax.axis_index("c").astype(jnp.int32).reshape(1)
     out = jax.ShapeDtypeStruct((tokens, head), dtype)
     return pl.pallas_call(
         finish_kernel,
         in_specs=[pl.BlockSpec(memory_space=pltpu.SMEM)]
-        + [pl.BlockSpec(memory_space=pltpu.VMEM)] * 5,
+        + [pl.BlockSpec(memory_space=pltpu.VMEM)] * 3,
         out_specs=[pl.BlockSpec(memory_space=pltpu.VMEM)] * 2 + [pl.BlockSpec(memory_space=pl.ANY)],
         out_shape=(out, out, jax.ShapeDtypeStruct((tokens, width), dtype)),
         scratch_shapes=[pltpu.VMEM((tokens, width), dtype), pltpu.SemaphoreType.DMA((count,))],
@@ -137,7 +146,7 @@
         cost_estimate=pl.CostEstimate(
             flops=8 * tokens * width * head, bytes_accessed=8 * tokens * width, transcendentals=0
         ),
-    )(core, activations, sheet, other_sheet, mine, other)
+    )(core, joined, sheet, other_sheet)
 
 
 def body(activations, w_query, w_key, grad_query, grad_key):
@@ -148,11 +157,10 @@
     near = 4 * ys * lows
     factor = 1.0 / math.sqrt(activations.shape[0] * 2 * near * highs)
 
-    mine = pick(grad_query, grad_key)
-    other = pick(grad_key, grad_query)
-    joined = jnp.concatenate([activations, other], axis=1)
+    core = lax.axis_index("c").astype(jnp.int32).reshape(1)
+    joined = jnp.concatenate([activations, grad_query, grad_key], axis=1)
     came = swap(joined, "c")
-    sent = terms(came, came, width, head, terms(joined, mine, width, head)).astype(jnp.float16)
+    sent = terms(core, came, width, head, terms(core, joined, width, head)).astype(jnp.float16)
     landed = exchange(sent.reshape((near,) + sent.shape[4:]), NEAR).astype(jnp.float32)
     summed = (landed[:, :-1] * jnp.exp2(-landed[:, -1:])).sum(axis=0)
 
@@ -173,7 +181,7 @@
     sheet = sheet.reshape(width, head)
     other_sheet = swap(sheet, "c")
 
-    query_out, key_out, grad_input = finish(activations, sheet, other_sheet, mine, other)
+    query_out, key_out, grad_input = finish(core, joined, sheet, other_sheet)
     return (query_out, key_out, grad_input, whole[0], whole[1])
 
 

time: 120 us -> 119 us (level)
  other arithmetic: 3.72 us -> 1.63 us
  local copies, waits for them, and re-layouts: 2.13 us -> 3.46 us
    unnamed x6 -> x10, local copies, waits for them, and re-layouts: 0.02 us -> 1.33 us
    concatenate x1 -> x0, other arithmetic: 1.3 us -> none  [body(): joined = jnp.concatenate([activations, other], axis=1)]
where the time goes in v8:
time: 119 us
  blocking collectives  42.7 us (36%)
  starting transfers between devices  39.9 us (34%)
  waiting for transfers between devices  26.5 us (22%)
  Pallas kernels  3.73 us (3%)
  local copies, waits for them, and re-layouts  3.46 us (3%)
  other arithmetic  1.63 us (1%)
    all_to_all x1, blocking collectives, exchange(): return lax.all_to_all(blocks, axes, 0, 0, tiled=True)  42.7 us
    ppermute x4, starting transfers between devices, swap(): return lax.ppermute(block, axis, [(0, 1), (1, 0)])  31.9 us
    all_to_all x2, waiting for transfers between devices, exchange(): return lax.all_to_all(blocks, axes, 0, 0, tiled=True)  20.5 us
    all_to_all x2, starting transfers between devices, exchange(): return lax.all_to_all(blocks, axes, 0, 0, tiled=True)  8 us
    ppermute x4, waiting for transfers between devices, swap(): return lax.ppermute(block, axis, [(0, 1), (1, 0)])  6.02 us
    pallas_call x1, Pallas kernels, finish(): pl.pallas_call(finish_kernel, in_specs=[pl.BlockSpec(memory_space=pltpu.S...  2.42 us
  transfers between devices with their start and end apart: 6, of which 6 were waited for; matrix products, arithmetic and copies ran while one was open for 1% of the time, Pallas kernels for 0%

profile of v8, /device:TPU:1, one launch (start us, length us, event | category | flops | bytes accessed | tf_op | source)
XLA Modules:
  0.0 118.8 jit_solution(8090534016307240031)
XLA Ops:
  0.7 1.3 %constant_dynamic-update-slice_fusion.2 = bf16[128,4352]{1,0:T(8,128)(2,1)S(1)} fusion(bf16[128,4096]{1,0:T(8,128)(2,1)} %param.5), kind=kLoop, calls=%fused_computation.16 | loop fusion | bytes 2097152
  2.0 16.1 %collective-permute-start = (bf16[128,4352]{1,0:T(8,128)(2,1)S(1)}, bf16[128,4352]{1,0:T(8,128)(2,1)S(1)}, u32[]{:S(2)}, u32[]{:S(2)}) collective-permute-start(bf16[128,4352]{1,0:T(8,128)(2,1)S(1)} %constant_dynamic-update-slice_fusion.refs_1_.joined_ref), channel_id=1, source_target_pairs={{0,256},{256,0},{1,257},{257,1},{2,258},{258,2},{3,259},{259,3},{4... | collective-permute-start | bytes 3342344 | tf_op jit(solution)/shard_map/ppermute | solution.py:14
  18.1 0.5 shard_map.92.refs_2_
  18.6 1.9 %collective-permute-done.refs_1_ = bf16[128,4352]{1,0:T(8,128)(2,1)S(1)} collective-permute-done((bf16[128,4352]{1,0:T(8,128)(2,1)S(1)}, bf16[128,4352]{1,0:T(8,128)(2,1)S(1)}, u32[]{:S(2)}, u32[]{:S(2)}) %collective-permute-start) | collective-permute-done | bytes 1114144 | tf_op jit(solution)/shard_map/ppermute | solution.py:14
  20.4 0.8 shard_map.93
  21.3 1.1 convert_element_type.15
  22.4 4.1 %all-to-all-start = ((f16[32,17,8,128]{3,2,1,0:T(8,128)(2,1)}), f16[32,17,8,128]{3,2,1,0:T(8,128)(2,1)S(1)}, u32[]{:S(2)}, u32[]{:S(2)}) async-start(f16[32,17,8,128]{3,2,1,0:T(8,128)(2,1)} %bitcast.1), calls=%async_computation | async-start | bytes 2228224 | tf_op jit(solution)/shard_map/all_to_all | solution.py:27
  26.5 0.0 copy-done.2
  26.6 18.2 %all-to-all-done = f16[32,17,8,128]{3,2,1,0:T(8,128)(2,1)S(1)} async-done(((f16[32,17,8,128]{3,2,1,0:T(8,128)(2,1)}), f16[32,17,8,128]{3,2,1,0:T(8,128)(2,1)S(1)}, u32[]{:S(2)}, u32[]{:S(2)}) %all-to-all-start) | async-done | bytes 1114144 | tf_op jit(solution)/shard_map/all_to_all | solution.py:27
  44.7 0.1 convert_element_type.16
  44.9 0.2 fusion
  45.2 42.7 %all_to_all.15 = bf16[16,24,128]{2,1,0:T(8,128)(2,1)S(1)} all-to-all(bf16[16,24,128]{2,1,0:T(8,128)(2,1)S(1)} %pad_maximum_fusion), channel_id=1, replica_groups=mesh['xh'=2,'c'=2,'y'=4,'zh'=16,'zl'=2,'xl'=2] {'zh'}, dimensions={0} | all-to-all | bytes 196608 | tf_op jit(solution)/shard_map/all_to_all | solution.py:27
  87.9 1.2 %broadcast_in_dim.5 = bf16[32,16,8,128]{3,2,1,0:T(8,128)(2,1)} broadcast(bf16[16,8,128]{2,1,0:T(8,128)(2,1)S(1)} %slice.34), dimensions={1,2,3} | broadcast | bytes 1081344 | tf_op jit(solution)/shard_map/broadcast_in_dim | solution.py:31
  89.1 3.9 %all-to-all-start.2 = ((bf16[32,16,8,128]{3,2,1,0:T(8,128)(2,1)}), bf16[32,16,8,128]{3,2,1,0:T(8,128)(2,1)S(1)}, u32[]{:S(2)}, u32[]{:S(2)}) async-start(bf16[32,16,8,128]{3,2,1,0:T(8,128)(2,1)} %broadcast_in_dim.5), calls=%async_computation.2 | async-start | bytes 2097152 | tf_op jit(solution)/shard_map/all_to_all | solution.py:27
  93.1 4.9 %collective-permute-start.1 = (f32[8,128]{1,0:T(8,128)S(1)}, f32[8,128]{1,0:T(8,128)S(1)}, u32[]{:S(2)}, u32[]{:S(2)}) collective-permute-start(f32[8,128]{1,0:T(8,128)S(1)} %broadcast_multiply_fusion), channel_id=1, source_target_pairs={{0,256},{256,0},{1,257},{257,1},{2,258},{258,2},{3,259},{259,3},{4... | collective-permute-start | bytes 12296 | tf_op jit(solution)/shard_map/ppermute | solution.py:14
  98.0 0.8 collective-permute-done.1
  98.8 4.9 %collective-permute-start.2 = (f32[2,8,128]{2,1,0:T(8,128)S(1)}, f32[2,8,128]{2,1,0:T(8,128)S(1)}, u32[]{:S(2)}, u32[]{:S(2)}) collective-permute-start(f32[2,8,128]{2,1,0:T(8,128)S(1)} %pad_maximum_fusion.2), channel_id=1, source_target_pairs={{0,512},{512,0},{1,513},{513,1},{2,514},{514,2},{3,515},{515,3},{4... | collective-permute-start | bytes 24584 | tf_op jit(solution)/shard_map/ppermute | solution.py:14
  103.7 1.7 %collective-permute-done.2 = f32[2,8,128]{2,1,0:T(8,128)S(1)} collective-permute-done((f32[2,8,128]{2,1,0:T(8,128)S(1)}, f32[2,8,128]{2,1,0:T(8,128)S(1)}, u32[]{:S(2)}, u32[]{:S(2)}) %collective-permute-start.2) | collective-permute-done | bytes 8224 | tf_op jit(solution)/shard_map/ppermute | solution.py:14
  105.4 2.3 %all-to-all-done.2 = bf16[32,16,8,128]{3,2,1,0:T(8,128)(2,1)S(1)} async-done(((bf16[32,16,8,128]{3,2,1,0:T(8,128)(2,1)}), bf16[32,16,8,128]{3,2,1,0:T(8,128)(2,1)S(1)}, u32[]{:S(2)}, u32[]{:S(2)}) %all-to-all-start.2) | async-done | bytes 1048608 | tf_op jit(solution)/shard_map/all_to_all | solution.py:27
  107.7 0.3 copy.10
  108.0 6.1 %collective-permute-start.3 = (bf16[4096,128]{1,0:T(8,128)(2,1)S(1)}, bf16[4096,128]{1,0:T(8,128)(2,1)S(1)}, u32[]{:S(2)}, u32[]{:S(2)}) collective-permute-start(bf16[4096,128]{1,0:T(8,128)(2,1)S(1)} %bitcast.16), channel_id=1, source_target_pairs={{0,256},{256,0},{1,257},{257,1},{2,258},{258,2},{3,259},{259,3},{4... | collective-permute-start | bytes 3145736 | tf_op jit(solution)/shard_map/ppermute | solution.py:14
  114.1 0.6 slice_bitcast_fusion
  114.7 1.7 %collective-permute-done.3.came_ref = bf16[4096,128]{1,0:T(8,128)(2,1)S(1)} collective-permute-done((bf16[4096,128]{1,0:T(8,128)(2,1)S(1)}, bf16[4096,128]{1,0:T(8,128)(2,1)S(1)}, u32[]{:S(2)}, u32[]{:S(2)}) %collective-permute-start.3) | collective-permute-done | bytes 1048608 | tf_op jit(solution)/shard_map/ppermute | solution.py:14
  116.4 2.4 %shard_map.94 = (bf16[128,128]{1,0:T(8,128)(2,1)}, bf16[128,128]{1,0:T(8,128)(2,1)}, bf16[128,4096]{1,0:T(8,128)(2,1)}) custom-call(s32[1]{0:T(128)} %bitcast.refs_0_.core_ref, bf16[128,4352]{1,0:T(8,128)(2,1)S(1)} %constant_dynamic-update-slice_fusion.refs_1_.joined_ref, bf16[4096,128]{1,0:T(8,128)(2,1)S(1)} %bitcast.17, ...), custom_call_target="tpu_custom_call" | custom-call | flops 536870912 | bytes 4194304 | tf_op jit(solution)/shard_map/pallas_call | solution.py:138
  (22 shorter events, 0.2 us)
Async XLA Ops:
  0.6 1.3 %copy-start = (bf16[128,128]{1,0:T(8,128)(2,1)S(1)}, bf16[128,128]{1,0:T(8,128)(2,1)}, u32[]{:S(2)}) copy-start(bf16[128,128]{1,0:T(8,128)(2,1)} %param.8) | copy-start | bytes 98308
  0.6 1.3 %copy-start.1 = (bf16[128,128]{1,0:T(8,128)(2,1)S(1)}, bf16[128,128]{1,0:T(8,128)(2,1)}, u32[]{:S(2)}) copy-start(bf16[128,128]{1,0:T(8,128)(2,1)} %param.9) | copy-start | bytes 98308
  2.0 18.4 %collective-permute-start = (bf16[128,4352]{1,0:T(8,128)(2,1)S(1)}, bf16[128,4352]{1,0:T(8,128)(2,1)S(1)}, u32[]{:S(2)}, u32[]{:S(2)}) collective-permute-start(bf16[128,4352]{1,0:T(8,128)(2,1)S(1)} %constant_dynamic-update-slice_fusion.refs_1_.joined_ref), channel_id=1, source_target_pairs={{0,256},{256,0},{1,257},{257,1},{2,258},{258,2},{3,259},{259,3},{4... | collective-permute-start | bytes 3342344 | tf_op jit(solution)/shard_map/ppermute | solution.py:14
  22.4 4.1 %copy-start.2 = (bf16[16,128]{1,0:T(8,128)(2,1)S(1)}, bf16[16,128]{1,0:T(8,128)(2,1)}, u32[]{:S(2)}) copy-start(bf16[16,128]{1,0:T(8,128)(2,1)} %param.7) | copy-start | bytes 12292
  22.4 4.1 %copy-start.3 = (bf16[16,128]{1,0:T(8,128)(2,1)S(1)}, bf16[16,128]{1,0:T(8,128)(2,1)}, u32[]{:S(2)}) copy-start(bf16[16,128]{1,0:T(8,128)(2,1)} %param.6) | copy-start | bytes 12292
  22.4 22.3 %all-to-all-start = ((f16[32,17,8,128]{3,2,1,0:T(8,128)(2,1)}), f16[32,17,8,128]{3,2,1,0:T(8,128)(2,1)S(1)}, u32[]{:S(2)}, u32[]{:S(2)}) async-start(f16[32,17,8,128]{3,2,1,0:T(8,128)(2,1)} %bitcast.1), calls=%async_computation | async-start | bytes 2228224 | tf_op jit(solution)/shard_map/all_to_all | solution.py:27
  89.1 18.6 %all-to-all-start.2 = ((bf16[32,16,8,128]{3,2,1,0:T(8,128)(2,1)}), bf16[32,16,8,128]{3,2,1,0:T(8,128)(2,1)S(1)}, u32[]{:S(2)}, u32[]{:S(2)}) async-start(bf16[32,16,8,128]{3,2,1,0:T(8,128)(2,1)} %broadcast_in_dim.5), calls=%async_computation.2 | async-start | bytes 2097152 | tf_op jit(solution)/shard_map/all_to_all | solution.py:27
  93.1 5.7 %collective-permute-start.1 = (f32[8,128]{1,0:T(8,128)S(1)}, f32[8,128]{1,0:T(8,128)S(1)}, u32[]{:S(2)}, u32[]{:S(2)}) collective-permute-start(f32[8,128]{1,0:T(8,128)S(1)} %broadcast_multiply_fusion), channel_id=1, source_target_pairs={{0,256},{256,0},{1,257},{257,1},{2,258},{258,2},{3,259},{259,3},{4... | collective-permute-start | bytes 12296 | tf_op jit(solution)/shard_map/ppermute | solution.py:14
  98.8 6.6 %collective-permute-start.2 = (f32[2,8,128]{2,1,0:T(8,128)S(1)}, f32[2,8,128]{2,1,0:T(8,128)S(1)}, u32[]{:S(2)}, u32[]{:S(2)}) collective-permute-start(f32[2,8,128]{2,1,0:T(8,128)S(1)} %pad_maximum_fusion.2), channel_id=1, source_target_pairs={{0,512},{512,0},{1,513},{513,1},{2,514},{514,2},{3,515},{515,3},{4... | collective-permute-start | bytes 24584 | tf_op jit(solution)/shard_map/ppermute | solution.py:14
  108.0 8.4 %collective-permute-start.3 = (bf16[4096,128]{1,0:T(8,128)(2,1)S(1)}, bf16[4096,128]{1,0:T(8,128)(2,1)S(1)}, u32[]{:S(2)}, u32[]{:S(2)}) collective-permute-start(bf16[4096,128]{1,0:T(8,128)(2,1)S(1)} %bitcast.16), channel_id=1, source_target_pairs={{0,256},{256,0},{1,257},{257,1},{2,258},{258,2},{3,259},{259,3},{4... | collective-permute-start | bytes 3145736 | tf_op jit(solution)/shard_map/ppermute | solution.py:14
